TPU v7x, 32 devices: a whole 2x2x4 slice. The times are simulated.
32 devices in a mesh: file: 16 (over z, y, core), win: 2 (over x).
Axes of the slice: x: 2, y: 2, z: 4, core: 2. Of those that a mesh axis runs over, the one named last changes fastest.
Arguments:
- raw: bfloat16 [2, 128, 20480], P('win', None, 'file'), may hold values from -60 to 60
- fir_taps: float32 [64], replicated, may hold values from -0.75 to 0.75
- offsets: int32 [2, 16], P('win', 'file'), may hold values from 0 to 9
- vs_index: int32 [64], replicated, may hold values from 0 to 127, as said below
Outputs:
- correlation: float32 [64, 128, 2048], P('win', 'file')
Inputs may be any that keep to these rules, and one draw needn't show every extreme that they name: `vs_index`: virtual source s is one of the channels s * 2 to s * 2 + 1.
All inputs are finite; a program needn't handle non-finite values.
Results may differ from a plain program's by a relative error of at most 0.0063.
Values may be sent and summed in bfloat16 or wider, within the bound.
No kernel may reach another device: no remote copies, remote signals or barrier semaphores. Data moves between devices by JAX's collectives and lax.ppermute only.
A program may use at most 128 MiB of HBM per device.

v0:
```python
import math

import jax
import jax.numpy as jnp
from jax import lax
from jax.sharding import PartitionSpec as P

R = 10
TAPS = 64
TD = 128
SEG = 2048
BAND = 64
VS_DEV = 4


PRECISE = lax.Precision.HIGHEST
EPSILON = 1e-06


def phase_table(height, breadth, period_len):
    row_index = lax.broadcasted_iota(jnp.int32, (height, breadth), 0)
    col_index = lax.broadcasted_iota(jnp.int32, (height, breadth), 1)
    residue = row_index * col_index % period_len
    angles = residue.astype(jnp.float32) * (2.0 * math.pi / period_len)
    return (jnp.cos(angles), jnp.sin(angles))


def forward_spectrum(samples):
    length = samples.shape[-1]
    factor = min(128, length)
    inner = length // factor
    outer = 2 * length // factor
    half_factor = factor // 2
    leading = samples.shape[:-1]
    arranged = samples.astype(jnp.float32).reshape(leading + (inner, factor))
    cos_a, sin_a = phase_table(inner, outer, outer)
    first_re = jnp.einsum("...pa,pm->...ma", arranged, cos_a, precision=PRECISE)
    first_im = -jnp.einsum("...pa,pm->...ma", arranged, sin_a, precision=PRECISE)
    cos_t, sin_t = phase_table(outer, factor, 2 * length)
    twist_re = first_re * cos_t + first_im * sin_t
    twist_im = first_im * cos_t - first_re * sin_t
    cos_b, sin_b = phase_table(factor, half_factor, factor)
    out_re = jnp.einsum("...ma,an->...nm", twist_re, cos_b, precision=PRECISE) + jnp.einsum(
        "...ma,an->...nm", twist_im, sin_b, precision=PRECISE
    )
    out_im = jnp.einsum("...ma,an->...nm", twist_im, cos_b, precision=PRECISE) - jnp.einsum(
        "...ma,an->...nm", twist_re, sin_b, precision=PRECISE
    )
    return (out_re.reshape(leading + (length,)), out_im.reshape(leading + (length,)))


def inverse_lags(cross_re, cross_im):
    length = cross_re.shape[-1]
    factor = min(128, length)
    inner = length // factor
    outer = 2 * length // factor
    half_factor = factor // 2
    leading = cross_re.shape[:-1]
    quarter = jnp.arange(length, dtype=jnp.int32) % 4
    rotate_c = jnp.where(quarter == 0, 1.0, jnp.where(quarter == 2, -1.0, 0.0)).astype(jnp.float32)
    rotate_s = jnp.where(quarter == 1, 1.0, jnp.where(quarter == 3, -1.0, 0.0)).astype(jnp.float32)
    turned_re = (cross_re * rotate_c + cross_im * rotate_s).reshape(leading + (inner, factor))
    turned_im = (cross_im * rotate_c - cross_re * rotate_s).reshape(leading + (inner, factor))
    cos_a, sin_a = phase_table(inner, outer, outer)
    first_re = jnp.einsum("...pa,pm->...ma", turned_re, cos_a, precision=PRECISE) - jnp.einsum(
        "...pa,pm->...ma", turned_im, sin_a, precision=PRECISE
    )
    first_im = jnp.einsum("...pa,pm->...ma", turned_re, sin_a, precision=PRECISE) + jnp.einsum(
        "...pa,pm->...ma", turned_im, cos_a, precision=PRECISE
    )
    cos_t, sin_t = phase_table(outer, factor, 2 * length)
    twist_re = first_re * cos_t - first_im * sin_t
    twist_im = first_re * sin_t + first_im * cos_t
    cos_b, sin_b = phase_table(factor, half_factor, factor)
    lagged = jnp.einsum("...ma,an->...nm", twist_re, cos_b, precision=PRECISE) - jnp.einsum(
        "...ma,an->...nm", twist_im, sin_b, precision=PRECISE
    )
    return lagged.reshape(leading + (length,))


def whiten(spec_re, spec_im):
    length = spec_re.shape[-1]
    leading = spec_re.shape[:-1]
    magnitude = jnp.sqrt(spec_re * spec_re + spec_im * spec_im)
    amplitude = (
        jnp.mean(magnitude.reshape(leading + (length // BAND, BAND)), axis=-1, keepdims=True)
        + EPSILON
    )
    white_re = (spec_re.reshape(leading + (length // BAND, BAND)) / amplitude).reshape(
        leading + (length,)
    )
    white_im = (spec_im.reshape(leading + (length // BAND, BAND)) / amplitude).reshape(
        leading + (length,)
    )
    return (white_re.astype(jnp.bfloat16), white_im.astype(jnp.bfloat16))


def band_matrix(fir_taps, block_width):
    span = R * block_width + TAPS - R
    period_len = span + R
    flipped = fir_taps[::-1].astype(jnp.bfloat16)
    pattern = jnp.concatenate([flipped, jnp.zeros((period_len - TAPS,), jnp.bfloat16)])
    flat = jnp.tile(pattern, block_width)[: block_width * span]
    return flat.reshape(block_width, span).T


def decimate(extended, offset_now, band_taps):
    row_count = extended.shape[0]
    block_width = band_taps.shape[1]
    span = R * (TD - 1) + TAPS
    segment = lax.dynamic_slice_in_dim(extended, offset_now + 1, span, axis=1)
    block_count = TD // block_width
    stride_len = R * block_width
    leading_part = segment[:, : stride_len * block_count].reshape(
        row_count, block_count, stride_len
    )
    trailing = segment[:, stride_len:]
    trailing = jnp.pad(trailing, ((0, 0), (0, stride_len * block_count - trailing.shape[1])))
    trailing = trailing.reshape(row_count, block_count, stride_len)[:, :, : TAPS - R]
    blocks = jnp.concatenate([leading_part, trailing], axis=2)
    result = jnp.einsum("cbi,io->cbo", blocks, band_taps, preferred_element_type=jnp.float32)
    return result.reshape(row_count, TD)


def local(raw, fir_taps, offsets, vs_index):
    samples = raw[0]
    file_count = lax.axis_size("file")
    win_count = lax.axis_size("win")
    band_taps = band_matrix(fir_taps, math.gcd(TD, 128))
    regrouped = lax.all_to_all(samples, "file", split_axis=0, concat_axis=1, tiled=True)
    shifts = lax.all_gather(offsets, "file", axis=1, tiled=True)
    row_count = regrouped.shape[0]
    file_blocks = regrouped.reshape(row_count, file_count, regrouped.shape[1] // file_count)
    previous = jnp.concatenate(
        [
            jnp.zeros((row_count, 1, TAPS), file_blocks.dtype),
            file_blocks[:, :-1, file_blocks.shape[2] - TAPS :],
        ],
        axis=1,
    )
    extended = jnp.concatenate([previous, file_blocks], axis=2)
    pieces = jax.vmap(decimate, in_axes=(1, 0, None), out_axes=1)(extended, shifts[0], band_taps)
    owned = pieces.reshape(row_count, file_count * TD).astype(jnp.bfloat16)
    row_count = owned.shape[0]
    seg_count = owned.shape[1] // SEG
    own_re, own_im = forward_spectrum(owned.reshape(row_count, seg_count, SEG))
    white_re, white_im = whiten(own_re, own_im)
    file_pos = lax.axis_index("file")
    source_rows = (
        lax.dynamic_slice_in_dim(vs_index, file_pos * VS_DEV, VS_DEV) - file_pos * row_count
    )
    source_re, source_im = (
        lax.all_gather(jnp.take(white_re, source_rows, axis=0), "file", axis=0, tiled=True),
        lax.all_gather(jnp.take(white_im, source_rows, axis=0), "file", axis=0, tiled=True),
    )
    own_both = jnp.concatenate([white_re, white_im], axis=1)
    scale_out = 1.0 / math.sqrt(SEG * seg_count * win_count)
    paired = jnp.stack(
        [
            jnp.concatenate([source_re, source_im], axis=1),
            jnp.concatenate([-source_im, source_re], axis=1),
        ],
        axis=1,
    )
    joined = jnp.einsum("cqf,sdqf->scdf", own_both, paired, preferred_element_type=jnp.float32)
    stacked = lax.psum_scatter(
        joined.reshape(joined.shape[0], joined.shape[1], 2 * SEG),
        "win",
        scatter_dimension=0,
        tiled=True,
    )
    return inverse_lags(stacked[..., :SEG], stacked[..., SEG:]) * scale_out


def solution(mesh):
    return jax.shard_map(
        local,
        mesh=mesh,
        in_specs=(P("win", None, "file"), P(), P("win", "file"), P()),
        out_specs=P("win", "file", None),
        check_vma=False,
    )
```

profile of v0, /device:TPU:0, one launch (start us, length us, event | category | flops | bytes accessed | tf_op | source)
XLA Modules:
  0.0 293.7 jit_solution(40036436673634234)
XLA Ops:
  6.5 7.4 %all-to-all-start = ((bf16[16,8,1280]{2,1,0:T(8,128)(2,1)}), bf16[16,8,1280]{2,1,0:T(8,128)(2,1)S(1)}, u32[]{:S(2)}, u32[]{:S(2)}) async-start(bf16[16,8,1280]{2,1,0:T(8,128)(2,1)} %bitcast.144), calls=%async_computation | async-start | bytes 655360 | tf_op jit(solution)/shard_map/all_to_all | solution.py:130
  17.3 12.4 %all-reduce.4 = s32[16]{0:T(128)S(1)} all-reduce(s32[16]{0:T(128)S(1)} %bitcast_dynamic-update-slice_fusion), channel_id=1, replica_groups=mesh['file'=16,'win'=2] {'file'}, use_global_device_ids=true, to_apply=%add.4 | all-reduce | flops 16 | bytes 128
  31.9 29.9 %while.1 = (s32[]{:T(128)}, bf16[16,8,1344]{2,1,0:T(8,128)(2,1)S(1)}, s32[16,3]{0,1:T(4,128)S(1)}, bf16[16,8,1334]{2,1,0:T(8,128)(2,1)S(1)}, s32[]{:T(128)}) while((s32[]{:T(128)}, bf16[16,8,1344]{2,1,0:T(8,128)(2,1)S(1)}, s32[16,3]{0,1:T(4,128)S(1)}, bf16[16,8,1334]{2,1,0:T(8,128)(2,1)S(1)}, s32[]{:T(128)}) %tuple.29), condition=%wide.while_cond, body=%wide.while_body.sunk | while | flops 2 | bytes 45173 | solution.py:111
  32.5 1.3 dynamic-slice_dynamic-update-slice_fusion.2
  34.4 1.3 dynamic-slice_dynamic-update-slice_fusion.2
  43.7 1.3 dynamic-slice_dynamic-update-slice_fusion.2
  49.4 1.3 dynamic-slice_dynamic-update-slice_fusion.2
  55.0 1.3 dynamic-slice_dynamic-update-slice_fusion.2
  67.5 19.4 %all_gather.11 = bf16[64,1,2048]{2,1,0:T(2,128)(2,1)S(1)} all-gather(bf16[4,1,2048]{2,1,0:T(2,128)(2,1)S(1)} %copy.77), channel_id=1, replica_groups=mesh['file'=16,'win'=2] {'file'}, dimensions={0}, use_global_device_ids=true | all-gather | bytes 278528 | tf_op jit(solution)/shard_map/all_gather | solution.py:154
  87.1 19.7 %all_gather.10 = bf16[64,1,2048]{2,1,0:T(2,128)(2,1)S(1)} all-gather(bf16[4,1,2048]{2,1,0:T(2,128)(2,1)S(1)} %copy.75), channel_id=1, replica_groups=mesh['file'=16,'win'=2] {'file'}, dimensions={0}, use_global_device_ids=true | all-gather | bytes 278528 | tf_op jit(solution)/shard_map/all_gather | solution.py:153
  108.2 4.5 %copy.82 = bf16[64,2,2,2048]{0,2,1,3:T(2,128)(2,1)S(1)} copy(bf16[64,2,2,2048]{3,0,2,1:T(8,128)(2,1)} %pad_maximum_fusion) | data formatting | bytes 2097152 | tf_op jit(solution)/shard_map/stack | solution.py:158
  112.7 6.9 %convolution_bitcast_fusion = f32[64,8,2,2048]{0,1,2,3:T(8,128)} fusion(bf16[64,2,2,2048]{0,2,1,3:T(2,128)(2,1)S(1)} %copy.82, bf16[8,2,2048,1]{0,1,3,2:T(2,128)(2,1)S(1)} %copy.91), kind=kOutput, calls=%fused_computation.4 | convolution fusion | flops 8388608 | bytes 9502720 | tf_op jit(solution)/shard_map/cqf,sdqf->scdf/dot_general | solution.py:165
  119.6 17.3 %copy.84 = f32[64,8,2,2048]{3,2,1,0:T(2,128)} copy(f32[64,8,2,2048]{0,1,2,3:T(8,128)} %convolution_bitcast_fusion) | data formatting | bytes 16777216 | tf_op jit(solution)/shard_map/cqf,sdqf->scdf/transpose | solution.py:165
  136.8 11.8 %reshape.235 = f32[64,8,4096]{2,1,0:T(8,128)} reshape(f32[64,8,2,2048]{3,2,1,0:T(2,128)} %copy.84) | data formatting | bytes 16777216 | tf_op jit(solution)/shard_map/reshape | solution.py:167
  148.7 97.1 %reduce-scatter.2.cloned.1.call-done = f32[32,8,4096]{2,1,0:T(8,128)} async-done(((f32[64,8,4096]{2,1,0:T(8,128)}), f32[32,8,4096]{2,1,0:T(8,128)}) %reduce-scatter.2.cloned.1.call-update) | async-done | bytes 4194320 | tf_op jit(solution)/shard_map/reduce_scatter | solution.py:166
  245.8 2.8 subtract_bitcast_fusion
  248.6 3.5 %fusion.20 = f32[32,32,8,128]{3,0,2,1:T(8,128)S(1)} fusion(f32[32,8,16,128]{3,1,2,0:T(8,128)S(1)} %get-tuple-element.29), kind=kOutput, calls=%fused_computation.28 | convolution fusion | flops 201333760 | bytes 6291456 | tf_op jit(solution)/shard_map/...pa,pm->...ma/dot_general | solution.py:65
  252.1 3.7 %fusion.18 = f32[32,32,8,128]{3,0,2,1:T(8,128)S(1)} fusion(f32[32,8,16,128]{3,1,2,0:T(8,128)S(1)} %get-tuple-element.29), kind=kOutput, calls=%fused_computation.26 | convolution fusion | flops 201333760 | bytes 6291456 | tf_op jit(solution)/shard_map/...pa,pm->...ma/dot_general | solution.py:68
  255.8 3.6 %convolution_subtract_fusion = f32[32,32,8,128]{3,0,2,1:T(8,128)S(1)} fusion(f32[32,32,8,128]{3,0,2,1:T(8,128)S(1)} %fusion.20, f32[32,8,16,128]{3,1,2,0:T(8,128)S(1)} %get-tuple-element.28), kind=kOutput, calls=%fused_computation.17 | convolution fusion | flops 202382336 | bytes 10485760 | tf_op jit(solution)/shard_map/...pa,pm->...ma/dot_general | solution.py:65
  259.4 4.2 %convolution_add_fusion = f32[32,32,8,128]{3,0,2,1:T(8,128)S(1)} fusion(f32[32,32,8,128]{3,0,2,1:T(8,128)S(1)} %fusion.18, f32[32,8,16,128]{3,1,2,0:T(8,128)S(1)} %get-tuple-element.28), kind=kOutput, calls=%fused_computation.16 | convolution fusion | flops 202382336 | bytes 10485760 | tf_op jit(solution)/shard_map/...pa,pm->...ma/dot_general | solution.py:68
  263.6 3.5 %fusion = f32[64,32,8,32]{0,3,2,1:T(8,128)S(1)} fusion(f32[32,32,8,128]{3,0,2,1:T(8,128)S(1)} %convolution_add_fusion, f32[32,32,8,128]{3,0,2,1:T(8,128)S(1)} %convolution_subtract_fusion, f32[32,128]{1,0:T(8,128)S(1)} %get-tuple-element.38, f32[32,128]{1,0:T(8,128)S(1)} %get-tuple-element.39), kind=kOutput, calls=%fused_computation.5 | convolution fusion | flops 808566784 | bytes 10518528 | tf_op jit(solution)/shard_map/...ma,an->...nm/dot_general | solution.py:75
  267.1 5.3 %multiply_bitcast_fusion = f32[32,8,64,32]{2,3,1,0:T(8,128)} fusion(f32[64,32,8,32]{0,3,2,1:T(8,128)S(1)} %fusion, f32[32,32,8,128]{3,0,2,1:T(8,128)S(1)} %convolution_add_fusion, f32[32,32,8,128]{3,0,2,1:T(8,128)S(1)} %convolution_subtract_fusion, f32[32,128]{1,0:T(8,128)S(1)} %get-tuple-element.38, f32[32,128]{1,0:T(8,128)S(1)} %get-tuple-element.39), kind=kOutput, calls=%fused_computation.9 | convolution fusion | flops 809615360 | bytes 12615680 | tf_op jit(solution)/shard_map/...ma,an->...nm/dot_general | solution.py:75
  272.4 6.9 %copy.89 = f32[32,8,64,32]{3,2,1,0:T(8,128)} copy(f32[32,8,64,32]{2,3,1,0:T(8,128)} %multiply_bitcast_fusion) | data formatting | bytes 4194304 | tf_op jit(solution)/shard_map/mul | solution.py:172
  279.3 7.5 %mul.267 = f32[32,8,2048]{2,1,0:T(8,128)} reshape(f32[32,8,64,32]{3,2,1,0:T(8,128)} %copy.89) | data formatting | bytes 4194304 | tf_op jit(solution)/shard_map/mul | solution.py:172
  (98 shorter events, 35.5 us)
Async XLA Ops:
  6.5 25.1 %all-to-all-start = ((bf16[16,8,1280]{2,1,0:T(8,128)(2,1)}), bf16[16,8,1280]{2,1,0:T(8,128)(2,1)S(1)}, u32[]{:S(2)}, u32[]{:S(2)}) async-start(bf16[16,8,1280]{2,1,0:T(8,128)(2,1)} %bitcast.144), calls=%async_computation | async-start | bytes 655360 | tf_op jit(solution)/shard_map/all_to_all | solution.py:130
  13.9 231.8 %reduce-scatter.2.cloned.1.call-start = ((), (), s32[]{:S(2)}) async-start(), calls=%async_computation.2 | async-start | bytes 12582912 | tf_op jit(solution)/shard_map/reduce_scatter | solution.py:166
Sparse Core Ops, SparseCore 0:
  148.8 96.9 reduce-scatter.1
where the time goes:
time: 295 us; the launch traced here: 294 us
  waiting for transfers between devices  97.1 us (33%)
  local copies, waits for them, and re-layouts  84.7 us (29%)
  blocking collectives  51.5 us (17%)
  matrix products  33.2 us (11%)
  between operations  14.4 us (5%)
  starting transfers between devices  7.43 us (3%)
  other arithmetic  5.31 us (2%)
    reduce_scatter x1, waiting for transfers between devices, local(): lax.psum_scatter(joined.reshape(joined.shape[0], joined.shape[1], 2 * SEG...  97.1 us
    gather x48, local copies, waits for them, and re-layouts  29.9 us
    all_gather x1, blocking collectives, local(): lax.all_gather(jnp.take(white_re, source_rows, axis=0), 'file', axis=0, t...  19.7 us
    all_gather x1, blocking collectives, local(): lax.all_gather(jnp.take(white_im, source_rows, axis=0), 'file', axis=0, t...  19.4 us
    transpose x1, local copies, waits for them, and re-layouts, local(): jnp.einsum('cqf,sdqf->scdf', own_both, paired, preferred_element_type=jnp...  17.3 us
    mul x2, local copies, waits for them, and re-layouts, local(): return inverse_lags(stacked[..., :SEG], stacked[..., SEG:]) * scale_out  14.4 us
    unnamed x1, blocking collectives  12.4 us
    reshape x1, local copies, waits for them, and re-layouts, local(): joined.reshape(joined.shape[0], joined.shape[1], 2 * SEG)  11.8 us
  transfers between devices with their start and end apart: 2, of which 1 were waited for; matrix products, arithmetic and copies ran while one was open for 2% of the time, Pallas kernels for 0%

commit v1 on v0

v1 whole, which is shorter than its diff:
```python
import functools
import math

import jax
import jax.numpy as jnp
import numpy as np
from jax import lax
from jax.experimental import pallas as pl
from jax.experimental.pallas import tpu as pltpu
from jax.sharding import PartitionSpec as P

R = 10
TAPS = 64
TD = 128
SEG = 2048
BAND = 64
EPSILON = 1e-06

PH = 16
LO = 256
NA = SEG // PH
NN = SEG // LO
HALF = LO // 128
SRC_BLOCKS = 2


def transform_tables():
    a = np.arange(NA)[:, None]
    m = np.arange(LO)[None, :]
    angle = 2 * np.pi * ((a * m) % LO) / LO
    cos, sin = np.cos(angle), np.sin(angle)
    forward = np.block([[cos.T, -sin.T], [sin.T, cos.T]])
    p = np.arange(PH)[:, None]
    turn = 2 * np.pi * (p * m) / (2 * SEG)
    full = 2 * np.pi * (((PH * a[None] + p[:, :, None]) * m[None]) % (2 * SEG)) / (2 * SEG)
    fc, fs = np.cos(full), np.sin(full)
    inverse = np.concatenate(
        [np.concatenate([fc, fs], axis=2), np.concatenate([-fs, fc], axis=2)], axis=1
    )
    lane = np.arange(NA)
    per_band = BAND // PH
    band = (lane[:, None] // per_band == lane[None, :] // per_band).astype(np.float32)
    return (
        jnp.asarray(forward, jnp.bfloat16),
        jnp.asarray(inverse, jnp.bfloat16),
        jnp.asarray(np.stack([np.cos(turn), np.sin(turn)]), jnp.float32),
        jnp.asarray(band, jnp.float32),
    )


def decimate_kernel(files, wins, offset_ref, taps_ref, index_ref, raw_ref, halo_ref, out_ref):
    channels = raw_ref.shape[0]
    half = TD // 2
    stride = R * half
    width = stride + 128
    offset = offset_ref[0, 0]
    taps = jnp.broadcast_to(taps_ref[...], (half, TAPS)).astype(jnp.bfloat16)
    k = lax.broadcasted_iota(jnp.int32, (TAPS, 256), 0)
    lane = lax.broadcasted_iota(jnp.int32, (TAPS, 256), 1)
    place = jnp.where(lane == 128 - k, 1.0, 0.0).astype(jnp.bfloat16)
    band = jnp.dot(taps, place, preferred_element_type=jnp.float32)
    shift = lax.broadcasted_iota(jnp.int32, (half, 128), 0) * R + offset
    wide_shift = jnp.concatenate([shift, shift], axis=1)
    for bit in range(7):
        band = jnp.where((wide_shift >> bit) % 2 == 1, pltpu.roll(band, 1 << bit, 1), band)
    tiles = []
    for t in range(width // 128):
        low = jnp.where(shift // 128 == t, band[:, :128], 0.0)
        tiles.append(low + jnp.where(shift // 128 == t - 1, band[:, 128:], 0.0))
    rolled = jnp.concatenate(tiles, axis=1).astype(jnp.bfloat16)
    nt = (((1,), (1,)), ((), ()))
    zero = jnp.zeros((half, width), jnp.bfloat16)
    first = jnp.concatenate([rolled, zero], axis=0)
    second = jnp.concatenate([zero, rolled], axis=0)
    total = lax.dot_general(
        raw_ref[:, stride - 128 : 2 * stride], second, nt, preferred_element_type=jnp.float32
    )
    total += lax.dot_general(
        raw_ref[:, :stride], first[:, 128:], nt, preferred_element_type=jnp.float32
    )
    total += lax.dot_general(halo_ref[...], first[:, :128], nt, preferred_element_type=jnp.float32)
    decimated = total.astype(jnp.bfloat16)
    sources = index_ref.shape[1]
    row = lax.broadcasted_iota(jnp.int32, (channels, sources), 0)
    pick = jnp.where(row == index_ref[...], 1.0, 0.0).astype(jnp.bfloat16)
    chosen = lax.dot_general(
        pick, decimated, (((0,), (0,)), ((), ())), preferred_element_type=jnp.float32
    ).astype(jnp.bfloat16)
    per_win = sources // wins
    per_file = channels // files
    for file in range(files):
        for win in range(wins):
            dest = file * wins + win
            out_ref[dest, :per_win, :] = chosen[win * per_win : (win + 1) * per_win]
            out_ref[dest, per_win:, :] = decimated[file * per_file : (file + 1) * per_file]


def spread(x):
    terms = []
    for p in range(PH // 2 + 1):
        re, im = None, None
        for n in range(NN):
            angle = (p * n) % PH
            c, s = math.cos(2 * math.pi * angle / PH), -math.sin(2 * math.pi * angle / PH)
            if angle % (PH // 4):
                re = x[n] * c if re is None else re + x[n] * c
                im = x[n] * s if im is None else im + x[n] * s
            elif angle % (PH // 2):
                im = x[n] * round(s) if im is None else (im + x[n] if s > 0 else im - x[n])
            else:
                re = x[n] if re is None else (re + x[n] if c > 0 else re - x[n])
        terms.append((re, jnp.zeros_like(re) if im is None else im))
    return terms


def gather_lags(re, im):
    half = PH // 2
    even = [None] + [re[p] + re[PH - p] for p in range(1, half)]
    odd = [None] + [im[p] - im[PH - p] for p in range(1, half)]
    quarter = half // 2
    both = [None] + [even[p] + even[half - p] for p in range(1, quarter)]
    apart = [None] + [even[p] - even[half - p] for p in range(1, quarter)]
    oboth = [None] + [odd[p] + odd[half - p] for p in range(1, quarter)]
    oapart = [None] + [odd[p] - odd[half - p] for p in range(1, quarter)]
    ends = (re[0] + re[half], re[0] - re[half])
    cosines, sines = {}, {}
    for n in range(NN // 2 + 1):
        fold, total = (both, ends[0]) if n % 2 == 0 else (apart, ends[1])
        if n % 2 == 0:
            total = total + even[quarter] if (n // 2) % 2 == 0 else total - even[quarter]
        for p in range(1, quarter):
            c = math.cos(2 * math.pi * p * n / PH)
            if abs(c) > 1e-9:
                total = total + (fold[p] if c == 1.0 else -fold[p] if c == -1.0 else fold[p] * c)
        cosines[n] = total
        if n:
            ofold = oapart if n % 2 == 0 else oboth
            total = None
            if n % 2:
                total = odd[quarter] if n % 4 == 1 else -odd[quarter]
            for p in range(1, quarter):
                s = math.sin(2 * math.pi * p * n / PH)
                if abs(s) > 1e-9:
                    term = ofold[p] * s
                    total = term if total is None else total + term
            sines[n] = total
    lags = []
    for n in range(-NN // 2, NN // 2):
        if n == 0:
            lags.append(cosines[0])
        elif sines[abs(n)] is None:
            lags.append(cosines[abs(n)])
        elif n < 0:
            lags.append(cosines[-n] + sines[-n])
        else:
            lags.append(cosines[n] - sines[n])
    return lags


def correlate_kernel(
    files, wins, sources, scale,
    data_ref, forward_ref, inverse_ref, turn_ref, band_ref, out_ref,
    z_ref, w_ref, pair_ref, lag_ref,
):
    rows = data_ref.shape[1]
    segs = files * TD // SEG
    per_seg = files // segs
    block = sources // SRC_BLOCKS
    chans = rows - sources
    groups = wins * segs

    @pl.when(pl.program_id(0) == 0)
    def _():
        for win in range(wins):
            for seg in range(segs):
                base = (win * segs + seg) * rows
                for h in range(HALF):
                    x = [
                        data_ref[(seg * per_seg + HALF * n + h) * wins + win].astype(jnp.float32)
                        for n in range(NN)
                    ]
                    terms = spread(x)
                    for p in range(PH):
                        re, im = terms[p] if p <= PH // 2 else terms[PH - p]
                        if p > PH // 2:
                            im = -im
                        c = turn_ref[0, p : p + 1, 128 * h : 128 * h + 128]
                        s = turn_ref[1, p : p + 1, 128 * h : 128 * h + 128]
                        z_ref[p, base : base + rows, 128 * h : 128 * h + 128] = (
                            re * c + im * s
                        ).astype(jnp.bfloat16)
                        z_ref[p, base : base + rows, LO + 128 * h : LO + 128 * h + 128] = (
                            im * c - re * s
                        ).astype(jnp.bfloat16)
        total = jnp.zeros((groups * rows, NA), jnp.float32)
        for p in range(PH):
            spec = jnp.dot(z_ref[p], forward_ref[...], preferred_element_type=jnp.float32)
            w_ref[p] = spec
            re, im = spec[:, :NA], spec[:, NA:]
            total += jnp.sqrt(re * re + im * im)
        amplitude = (
            jnp.dot(
                total, band_ref[...], precision=lax.Precision.HIGHEST,
                preferred_element_type=jnp.float32,
            )
            * (1.0 / BAND)
            + EPSILON
        )
        gain = 1.0 / amplitude
        gain = jnp.concatenate([gain, gain], axis=1)
        for p in range(PH):
            w_ref[p] = (w_ref[p] * gain).astype(jnp.bfloat16).astype(jnp.float32)

    first = pl.program_id(0) * block

    def one_phase(p, _):
        own = [
            (
                w_ref[p, g * rows + sources : (g + 1) * rows, :NA],
                w_ref[p, g * rows + sources : (g + 1) * rows, NA:],
            )
            for g in range(groups)
        ]

        def pair(s):
            cre, cim = None, None
            for g in range(groups):
                row = w_ref[p, pl.ds(g * rows + first + s, 1), :]
                sre = jnp.broadcast_to(row[:, :NA], (chans, NA))
                sim = jnp.broadcast_to(row[:, NA:], (chans, NA))
                ore, oim = own[g]
                tre = ore * sre + oim * sim
                tim = oim * sre - ore * sim
                cre = tre if cre is None else cre + tre
                cim = tim if cim is None else cim + tim
            return cre, cim

        for s in range(0, block, 2):
            r0, i0 = pair(s)
            r1, i1 = pair(s + 1)
            pair_ref[s * chans : (s + 2) * chans, :NA] = jnp.concatenate([r0, r1], 0).astype(jnp.bfloat16)
            pair_ref[s * chans : (s + 2) * chans, NA:] = jnp.concatenate([i0, i1], 0).astype(jnp.bfloat16)
        lag_ref[p] = jnp.dot(pair_ref[...], inverse_ref[p], preferred_element_type=jnp.float32)
        return 0

    lax.fori_loop(0, PH, one_phase, 0)

    def one_source(s, _):
        at = pl.ds(pl.multiple_of(s * chans, chans), chans)
        for h in range(HALF):
            lo = 128 * h
            re = [lag_ref[p, at, lo : lo + 128] for p in range(PH)]
            im = [lag_ref[p, at, LO + lo : LO + lo + 128] for p in range(PH)]
            for n, value in enumerate(gather_lags(re, im)):
                out_ref[s, :, LO * n + lo : LO * n + lo + 128] = value * scale
        return 0

    lax.fori_loop(0, block, one_source, 0)


def local(raw, fir_taps, offsets, vs_index):
    samples = raw[0]
    channels = samples.shape[0]
    files = lax.axis_size("file")
    wins = lax.axis_size("win")
    sources = vs_index.shape[0] // wins
    chans = channels // files
    rows = sources + chans
    segs = files * TD // SEG
    halo = lax.ppermute(
        samples[:, samples.shape[1] - 128 :], "file", [(i, i + 1) for i in range(files - 1)]
    )
    vmem = pl.BlockSpec(memory_space=pltpu.VMEM)
    packed = pl.pallas_call(
        functools.partial(decimate_kernel, files, wins),
        out_shape=jax.ShapeDtypeStruct((files * wins, rows, TD), jnp.bfloat16),
        in_specs=[pl.BlockSpec(memory_space=pltpu.SMEM), vmem, vmem, vmem, vmem],
        out_specs=vmem,
        compiler_params=pltpu.CompilerParams(vmem_limit_bytes=32 * 2**20),
        name="decimate",
    )(offsets, fir_taps[None, :], vs_index[None, :], samples, halo)
    data = lax.all_to_all(packed, ("file", "win"), split_axis=0, concat_axis=0, tiled=True)
    forward, inverse, turn, band = transform_tables()
    groups = wins * segs
    block = sources // SRC_BLOCKS
    scale = 1.0 / math.sqrt(SEG * segs * wins)
    whole = lambda shape: pl.BlockSpec(shape, lambda i: (0,) * len(shape))
    return pl.pallas_call(
        functools.partial(correlate_kernel, files, wins, sources, scale),
        grid=(SRC_BLOCKS,),
        out_shape=jax.ShapeDtypeStruct((sources, chans, SEG), jnp.float32),
        in_specs=[whole(x.shape) for x in (data, forward, inverse, turn, band)],
        out_specs=pl.BlockSpec((block, chans, SEG), lambda i: (i, 0, 0)),
        scratch_shapes=[
            pltpu.VMEM((PH, groups * rows, 2 * LO), jnp.bfloat16),
            pltpu.VMEM((PH, groups * rows, 2 * NA), jnp.float32),
            pltpu.VMEM((block * chans, 2 * NA), jnp.bfloat16),
            pltpu.VMEM((PH, block * chans, 2 * LO), jnp.float32),
        ],
        compiler_params=pltpu.CompilerParams(vmem_limit_bytes=56 * 2**20),
        name="correlate",
    )(data, forward, inverse, turn, band)


def solution(mesh):
    return jax.shard_map(
        local,
        mesh=mesh,
        in_specs=(P("win", None, "file"), P(), P("win", "file"), P()),
        out_specs=P("win", "file", None),
        check_vma=False,
    )
```

time: 295 us -> 40.8 us (0.14)
  waiting for transfers between devices: 97.1 us -> 0.19 us
  local copies, waits for them, and re-layouts: 84.7 us -> 3.04 us
  matrix products: 33.2 us -> 0 us
  blocking collectives: 51.5 us -> 21 us
  between operations: 14.4 us -> 0.67 us
  Pallas kernels: 0 us -> 13.3 us
  other arithmetic: 5.31 us -> 0 us
  starting transfers between devices: 7.43 us -> 2.35 us
    reduce_scatter x1 -> x0, waiting for transfers between devices: 97.1 us -> none  [local(): lax.psum_scatter(joined.reshape(joined.shape[0], joined.shape[1], 2 * SEG...]
    all_gather x2 -> x0, blocking collectives: 39.1 us -> none  [the longest x1 19.7 us: local(): lax.all_gather(jnp.take(white_re, source_rows, axis=0), 'file', axis=0, t...]
    dot_general x14 -> x0, matrix products: 33.2 us -> none  [the longest x1 6.88 us: local(): jnp.einsum('cqf,sdqf->scdf', own_both, paired, preferred_element_type=jnp...]
    gather x50 -> x0, local copies, waits for them, and re-layouts: 31 us -> none
    all_to_all x0 -> x1, blocking collectives: none -> 21 us  [local(): lax.all_to_all(packed, ('file', 'win'), split_axis=0, concat_axis=0, tile...]
    transpose x1 -> x0, local copies, waits for them, and re-layouts: 17.3 us -> none  [local(): jnp.einsum('cqf,sdqf->scdf', own_both, paired, preferred_element_type=jnp...]
    mul x2 -> x0, local copies, waits for them, and re-layouts: 14.4 us -> none  [local(): return inverse_lags(stacked[..., :SEG], stacked[..., SEG:]) * scale_out]
    pallas_call x0 -> x2, Pallas kernels: none -> 13.3 us  [the longest x1 12.3 us: local(): pl.pallas_call(functools.partial(correlate_kernel, files, wins, sources,...]
  transfers between devices with their start and end apart: 2 -> 1, of which waited for: 1 -> 1; matrix products, arithmetic and copies ran while one was open for 2% -> 0% of each run, Pallas kernels for 0% -> 0%
where the time goes in v1:
time: 40.8 us; the launch traced here: 40.5 us
  blocking collectives  21 us (51%)
  Pallas kernels  13.3 us (33%)
  local copies, waits for them, and re-layouts  3.04 us (7%)
  starting transfers between devices  2.35 us (6%)
  between operations  0.67 us (2%)
    all_to_all x1, blocking collectives, local(): lax.all_to_all(packed, ('file', 'win'), split_axis=0, concat_axis=0, tile...  21 us
    pallas_call x1, Pallas kernels, local(): pl.pallas_call(functools.partial(correlate_kernel, files, wins, sources,...  12.3 us
    ppermute x1, starting transfers between devices, local(): lax.ppermute(samples[:, samples.shape[1] - 128:], 'file', [(i, i + 1) for...  2.35 us
    unnamed x6, local copies, waits for them, and re-layouts  2.28 us
    pallas_call x1, Pallas kernels, local(): pl.pallas_call(functools.partial(decimate_kernel, files, wins), out_shape...  1.03 us
  transfers between devices with their start and end apart: 1, of which 1 were waited for; matrix products, arithmetic and copies ran while one was open for 0% of the time, Pallas kernels for 0%

profile of v1, /device:TPU:0, one launch (start us, length us, event | category | flops | bytes accessed | tf_op | source)
XLA Modules:
  0.0 40.5 jit_solution(10206059763869439202)
XLA Ops:
  0.0 0.8 %slice.4 = bf16[128,128]{1,0:T(8,128)(2,1)S(1)} slice(bf16[128,1280]{1,0:T(8,128)(2,1)} %bitcast.3), slice={[0:128], [1152:1280]} | slice | bytes 65536 | tf_op jit(solution)/shard_map/slice | solution.py:271
  0.8 2.3 %collective-permute-start = (bf16[128,128]{1,0:T(8,128)(2,1)S(1)}, bf16[128,128]{1,0:T(8,128)(2,1)S(1)}, u32[]{:S(2)}, u32[]{:S(2)}) collective-permute-start(bf16[128,128]{1,0:T(8,128)(2,1)S(1)} %slice.4), channel_id=1, source_target_pairs={{0,2},{2,4},{4,6},{6,8},{8,10},{10,12},{12,14},{14,16},{16,18},{18... | collective-permute-start | bytes 98312 | tf_op jit(solution)/shard_map/ppermute | solution.py:270
  3.8 0.2 collective-permute-done.halo_ref
  4.0 0.0 copy-start
  4.0 1.0 %copy-done = bf16[1,128,1280]{2,1,0:T(8,128)(2,1)S(1)} copy-done((bf16[1,128,1280]{2,1,0:T(8,128)(2,1)S(1)}, bf16[1,128,1280]{2,1,0:T(8,128)(2,1)}, u32[]{:S(2)}) %copy-start) | copy-done | bytes 327704
  4.9 0.0 copy-start.1
  4.9 0.7 %copy-done.1 = f32[64]{0:T(128)S(1)} copy-done((f32[64]{0:T(128)S(1)}, f32[64]{0:T(128)}, u32[]{:S(2)}) %copy-start.1) | copy-done | bytes 280
  5.6 0.0 copy-start.2
  5.6 0.7 %copy-done.2 = s32[64]{0:T(128)S(1)} copy-done((s32[64]{0:T(128)S(1)}, s32[64]{0:T(128)}, u32[]{:S(2)}) %copy-start.2) | copy-done | bytes 280
  6.2 1.0 %decimate.1 = bf16[32,40,128]{2,1,0:T(8,128)(2,1)S(1)} custom-call(s32[1,1]{1,0:T(1,128)S(6)} %copy.9.offset_ref, f32[1,64]{1,0:T(1,128)S(1)} %bitcast.5, s32[1,64]{1,0:T(1,128)S(1)} %bitcast.6, bf16[128,1280]{1,0:T(8,128)(2,1)S(1)} %bitcast.4, bf16[128,128]{1,0:T(8,128)(2,1)S(1)} %collective-permute-done.halo_ref), custom_call_target="tpu_custom_call" | custom-call | tf_op jit(solution)/shard_map/decimate/pallas_call | solution.py:274
  7.3 21.0 %all_to_all.5.data_ref = bf16[32,40,128]{2,1,0:T(8,128)(2,1)} all-to-all(bf16[32,40,128]{2,1,0:T(8,128)(2,1)S(1)} %decimate.1), channel_id=1, replica_groups=mesh['file'=16,'win'=2] {'file','win'}, dimensions={0} | all-to-all | bytes 655360 | tf_op jit(solution)/shard_map/all_to_all | solution.py:282
  28.2 12.3 %correlate.1 = f32[32,8,2048]{2,1,0:T(8,128)} custom-call(bf16[32,40,128]{2,1,0:T(8,128)(2,1)} %all_to_all.5.data_ref, bf16[512,256]{1,0:T(8,128)(2,1)} %constant.8.clone.forward_ref, bf16[16,256,512]{2,1,0:T(8,128)(2,1)} %constant.9.clone.inverse_ref, f32[2,16,256]{2,1,0:T(8,128)} %constant.10.clone.turn_ref, f32[128,128]{1,0:T(8,128)} %constant.11.clone.band_ref), custom_call_target="tpu_custom_call" | custom-call | tf_op jit(solution)/shard_map/correlate/pallas_call | solution.py:288
Async XLA Ops:
  0.8 3.2 %collective-permute-start = (bf16[128,128]{1,0:T(8,128)(2,1)S(1)}, bf16[128,128]{1,0:T(8,128)(2,1)S(1)}, u32[]{:S(2)}, u32[]{:S(2)}) collective-permute-start(bf16[128,128]{1,0:T(8,128)(2,1)S(1)} %slice.4), channel_id=1, source_target_pairs={{0,2},{2,4},{4,6},{6,8},{8,10},{10,12},{12,14},{14,16},{16,18},{18... | collective-permute-start | bytes 98312 | tf_op jit(solution)/shard_map/ppermute | solution.py:270
  4.0 1.0 %copy-start = (bf16[1,128,1280]{2,1,0:T(8,128)(2,1)S(1)}, bf16[1,128,1280]{2,1,0:T(8,128)(2,1)}, u32[]{:S(2)}) copy-start(bf16[1,128,1280]{2,1,0:T(8,128)(2,1)} %param.8) | copy-start | bytes 983044
  4.9 0.7 %copy-start.1 = (f32[64]{0:T(128)S(1)}, f32[64]{0:T(128)}, u32[]{:S(2)}) copy-start(f32[64]{0:T(128)} %param.9) | copy-start | bytes 772
  5.6 0.7 %copy-start.2 = (s32[64]{0:T(128)S(1)}, s32[64]{0:T(128)}, u32[]{:S(2)}) copy-start(s32[64]{0:T(128)} %param.11) | copy-start | bytes 772

commit v2 on v1

v2 whole, which is shorter than its diff:
```python
import functools
import math

import jax
import jax.numpy as jnp
import numpy as np
from jax import lax
from jax.experimental import pallas as pl
from jax.experimental.pallas import tpu as pltpu
from jax.sharding import PartitionSpec as P

R = 10
TAPS = 64
TD = 128
SEG = 2048
BAND = 64
EPSILON = 1e-06

PH = 16
LO = 256
NA = SEG // PH
NN = SEG // LO
HALF = LO // 128
PAIRS = PH // 2
EARLY = 8
GROUP = 4

NT = (((1,), (1,)), ((), ()))
NN_DIMS = (((1,), (0,)), ((), ()))
F32 = jnp.float32
BF16 = jnp.bfloat16


def split_table(x):
    high = x.astype(BF16)
    return np.stack([high, (x - high.astype(np.float64)).astype(BF16)])


def transform_table():
    a = np.arange(NA)[:, None]
    m = np.arange(LO)[None, :]

    def wave(f):
        angle = 2 * np.pi * ((f * m) % (2 * SEG)) / (2 * SEG)
        return np.cos(angle), np.sin(angle)

    c, s = wave(PH * a)
    cc, ss = wave(PH * (a + 1))
    folded = np.block([[c, s], [-s, c], [cc, -ss], [-ss, -cc]])
    c8, s8 = wave(PH * a + PH // 2)
    z = np.zeros_like(c)
    ends = np.block([[c, z], [-s, z], [z, c8], [z, -s8]])
    return jnp.asarray(split_table(np.stack([ends, folded])))


def three_pass(high, low, table_high, table_low, dims):
    dot = functools.partial(lax.dot_general, dimension_numbers=dims, preferred_element_type=F32)
    return dot(high, table_high) + (dot(low, table_high) + dot(high, table_low))


def split(x):
    high = x.astype(BF16)
    return high, (x - high.astype(F32)).astype(BF16)


def decimate_kernel(
    files, wins,
    offset_hbm, taps_hbm, index_hbm, raw_hbm, out_ref,
    offset_ref, taps_ref, index_ref, raw_ref, sems,
):
    copies = [
        pltpu.make_async_copy(source, target, sems.at[i])
        for i, (source, target) in enumerate(
            (
                (offset_hbm, offset_ref),
                (taps_hbm, taps_ref),
                (index_hbm, index_ref),
                (raw_hbm, raw_ref),
            )
        )
    ]
    for copy in copies:
        copy.start()
    channels, samples = raw_ref.shape
    half = TD // 2
    stride = R * half
    width = stride + 128
    copies[0].wait()
    copies[1].wait()
    offset = offset_ref[0, 0]
    taps = jnp.broadcast_to(taps_ref[...], (half, TAPS)).astype(BF16)
    k = lax.broadcasted_iota(jnp.int32, (TAPS, 256), 0)
    lane = lax.broadcasted_iota(jnp.int32, (TAPS, 256), 1)
    place = jnp.where(lane == 128 - k, 1.0, 0.0).astype(BF16)
    band = jnp.dot(taps, place, preferred_element_type=F32)
    shift = lax.broadcasted_iota(jnp.int32, (half, 128), 0) * R + offset
    wide_shift = jnp.concatenate([shift, shift], axis=1)
    for bit in range(7):
        band = jnp.where((wide_shift >> bit) % 2 == 1, pltpu.roll(band, 1 << bit, 1), band)
    tiles = []
    for t in range(width // 128):
        low = jnp.where(shift // 128 == t, band[:, :128], 0.0)
        tiles.append(low + jnp.where(shift // 128 == t - 1, band[:, 128:], 0.0))
    rolled = jnp.concatenate(tiles, axis=1).astype(BF16)
    zero = jnp.zeros((half, width), BF16)
    first = jnp.concatenate([rolled, zero], axis=0)
    second = jnp.concatenate([zero, rolled], axis=0)
    copies[2].wait()
    sources = index_ref.shape[1]
    row = lax.broadcasted_iota(jnp.int32, (channels, sources), 0)
    pick = jnp.where(row == index_ref[...], 1.0, 0.0).astype(BF16)
    copies[3].wait()
    total = lax.dot_general(
        raw_ref[:, stride - 128 : 2 * stride], second, NT, preferred_element_type=F32
    )
    total += lax.dot_general(raw_ref[:, :stride], first[:, 128:], NT, preferred_element_type=F32)
    decimated = total.astype(BF16)
    lane = lax.broadcasted_iota(jnp.int32, (channels, 128), 1)
    low = jnp.where(lane < EARLY, total - decimated.astype(F32), 0.0)
    tail = raw_ref[:, samples - 128 :].astype(F32)
    tail = jnp.where(lane == TAPS, offset.astype(F32), tail)
    everything = jnp.concatenate([decimated, tail.astype(BF16), low.astype(BF16)], axis=1)
    chosen = lax.dot_general(
        pick, everything, (((0,), (0,)), ((), ())), preferred_element_type=F32
    )
    per_win = sources // wins
    share = per_win // 2
    per_file = channels // files
    lower = lane[:per_file] < 64

    def low_lanes(value, i):
        return pltpu.roll(value, 64 + EARLY * i, 1)

    wide = jnp.concatenate([taps_ref[...], jnp.zeros((1, 128 - TAPS), F32)], axis=1)
    row = lax.broadcasted_iota(jnp.int32, (per_file, 128), 0)
    carried = jnp.where(row == 0, pltpu.roll(wide, 96, 1), pltpu.roll(wide, 64, 1))
    carried = jnp.where((row < 2) & (lane[:per_file] >= 96), carried, 0.0)
    blocks = {}
    for win in range(wins):
        for core in range(2):
            at = win * per_win + core * share
            part = chosen[at : at + share]
            tails = pltpu.roll(part[:, 128:256], 64, 1)
            lows = part[:, 256:]
            packed = carried + low_lanes(lows[:per_file], 0)
            for i in range(1, share // per_file):
                packed += low_lanes(lows[i * per_file : (i + 1) * per_file], i)
            second = tails[per_file:] if share > per_file else jnp.zeros_like(packed)
            blocks[win, core] = (
                part[:, :128].astype(BF16), tails[:per_file], jnp.where(lower, second, packed)
            )
    for file in range(files):
        own = slice(file * per_file, (file + 1) * per_file)
        own_low = low_lanes(low[own], share // per_file)
        for win in range(wins):
            dest = file * wins + win
            dec, tails, packed = blocks[win, file % 2]
            out_ref[dest, : 2 * per_file, :] = jnp.concatenate(
                [jnp.where(lower, tails, tail[own]), packed + own_low], axis=0
            ).astype(BF16)
            out_ref[dest, 2 * per_file : 2 * per_file + share, :] = dec
            out_ref[dest, 2 * per_file + share :, :] = decimated[own]


def spread(x):
    terms = []
    for p in range(PH // 2 + 1):
        re, im = None, None
        for n in range(NN):
            angle = (p * n) % PH
            c, s = math.cos(2 * math.pi * angle / PH), -math.sin(2 * math.pi * angle / PH)
            if angle % (PH // 4):
                re = x[n] * c if re is None else re + x[n] * c
                im = x[n] * s if im is None else im + x[n] * s
            elif angle % (PH // 2):
                im = x[n] * round(s) if im is None else (im + x[n] if s > 0 else im - x[n])
            else:
                re = x[n] if re is None else (re + x[n] if c > 0 else re - x[n])
        terms.append((re, im))
    return terms


def forward_kernel(
    files, wins, chans, scale,
    data_ref, table_hbm, own_ref, src_ref, table_ref, turn_ref,
    rest_ref, fixed_ref, high_ref, low_ref, spec_ref, sems,
):
    copies = [
        pltpu.make_async_copy(source, target, sems.at[i])
        for i, (source, target) in enumerate(
            ((table_hbm.at[0], table_ref), (table_hbm.at[1], rest_ref))
        )
    ]
    for copy in copies:
        copy.start()
    phase = lax.broadcasted_iota(jnp.int32, (8, LO), 0) * lax.broadcasted_iota(jnp.int32, (8, LO), 1)
    angle = phase.astype(F32) * (math.pi / SEG)
    turns = (jnp.cos(angle), jnp.sin(angle))
    for p in range(PAIRS):
        for i in range(2):
            turn_ref[i, p] = jnp.broadcast_to(turns[i][p : p + 1], (8, LO))
    rows = fixed_ref.shape[1]
    share = rows - chans
    lead = 2 * chans
    segs = files * TD // SEG
    per_seg = files // segs
    devices = files * wins

    first = data_ref[0, chans : 2 * chans, :].astype(F32)
    row = lax.broadcasted_iota(jnp.int32, (TAPS, 128), 0)
    lane = lax.broadcasted_iota(jnp.int32, (TAPS, 128), 1)
    taps = jnp.where(lane[:1] < 32, pltpu.roll(first[:1], 32, 1), pltpu.roll(first[1:2], 64, 1))
    share_of = jnp.where(lane < TAPS, jnp.broadcast_to(taps, (TAPS, 128)), 0.0)
    for bit in range(6):
        move = (TAPS - row) >> bit
        share_of = jnp.where(move % 2 == 1, pltpu.roll(share_of, 128 - (1 << bit), 1), share_of)
    share_of = jnp.where((lane < row) & (row > 0), share_of, 0.0).astype(BF16)
    nothing = jnp.zeros((TAPS, 128), BF16)
    row = lax.broadcasted_iota(jnp.int32, (128, 128), 0)
    lane = lax.broadcasted_iota(jnp.int32, (128, 128), 1)
    columns = [
        jnp.concatenate([share_of, nothing], axis=0),
        jnp.concatenate([nothing, share_of], axis=0),
        jnp.where(row == 0, 1.0, 0.0).astype(BF16),
    ]
    for i in range(rows // chans):
        columns.append(
            jnp.where((row == 64 + EARLY * i + lane) & (lane < EARLY), 1.0, 0.0).astype(BF16)
        )
    collapse = jnp.where((row // R == lane) & (lane < EARLY), 1.0, 0.0).astype(BF16)
    tails = data_ref[:, :lead, :].reshape(devices * lead, 128)
    mixed = jnp.dot(tails, jnp.concatenate(columns, axis=1), preferred_element_type=F32)
    mixed = mixed.reshape(devices, lead, len(columns) * 128)
    residue = (lax.broadcasted_iota(jnp.int32, (1, 1, 128), 2) % R).astype(F32)
    offset = mixed[wins:, :, 256:384]

    def early(value, kept):
        value = jnp.where(residue == offset[:, :kept], value[:-wins, :kept], 0.0)
        value = value.reshape((devices - wins) * kept, 128)
        high, low = split(value)
        value = jnp.dot(high, collapse, preferred_element_type=F32) + jnp.dot(
            low, collapse, preferred_element_type=F32
        )
        value = value.reshape(devices - wins, kept, 128)
        return jnp.concatenate([jnp.zeros((wins, kept, 128), F32), value], axis=0)

    added = jnp.concatenate(
        [early(mixed[:, :, :128], share), early(mixed[:, :, 128:256], chans)], axis=1
    )
    lows = jnp.concatenate(
        [
            mixed[:, chans:, 128 * (3 + i) : 128 * (4 + i)]
            for i in range(rows // chans)
        ],
        axis=1,
    )
    fixed_ref[...] = (data_ref[:, lead:, :].astype(F32) + (lows + added)).astype(BF16).astype(F32)

    for win in range(wins):
        for seg in range(segs):
            base = (win * segs + seg) * rows
            for h in range(HALF):
                x = [fixed_ref[(seg * per_seg + HALF * n + h) * wins + win] for n in range(NN)]
                terms = spread(x)
                for p in range(PAIRS):
                    if p:
                        re, im = terms[p]
                        c = turn_ref[0, p, :1, 128 * h : 128 * h + 128]
                        s = turn_ref[1, p, :1, 128 * h : 128 * h + 128]
                        re, im = re * c + im * s, im * c - re * s
                    else:
                        re, im = terms[0][0], terms[PAIRS][0]
                    for part, value in enumerate((re, im)):
                        at = slice(LO * part + 128 * h, LO * part + 128 * h + 128)
                        high, low = split(value)
                        high_ref[p, base : base + rows, at] = high
                        low_ref[p, base : base + rows, at] = low
    groups = wins * segs
    count = groups * rows
    for copy in copies:
        copy.wait()
    spec_ref[0] = three_pass(high_ref[0], low_ref[0], table_ref[0], rest_ref[0], NT)
    spec_ref[1:] = three_pass(
        high_ref[1:].reshape((PAIRS - 1) * count, 2 * LO),
        low_ref[1:].reshape((PAIRS - 1) * count, 2 * LO),
        table_ref[1],
        rest_ref[1],
        NT,
    ).reshape(PAIRS - 1, count, 4 * NA)
    total = jnp.zeros((count, NA), F32)
    for p in range(PAIRS):
        for part in range(2):
            re = spec_ref[p, :, 2 * NA * part : 2 * NA * part + NA]
            im = spec_ref[p, :, 2 * NA * part + NA : 2 * NA * part + 2 * NA]
            total += jnp.sqrt(re * re + im * im)
    high, low = split(total)
    low2 = (total - high.astype(F32) - low.astype(F32)).astype(BF16)
    row = lax.broadcasted_iota(jnp.int32, (NA, NA), 0)
    lane = lax.broadcasted_iota(jnp.int32, (NA, NA), 1)
    per_band = BAND // PH
    band = jnp.where(row // per_band == lane // per_band, 1.0, 0.0).astype(BF16)
    amplitude = (
        jnp.dot(high, band, preferred_element_type=F32)
        + jnp.dot(low, band, preferred_element_type=F32)
        + jnp.dot(low2, band, preferred_element_type=F32)
    ) * (1.0 / BAND) + EPSILON
    gain = 1.0 / amplitude
    gain = jnp.concatenate([gain] * 4, axis=1)
    for p in range(PAIRS):
        white = (spec_ref[p] * gain).astype(BF16)
        for group in range(groups):
            src_ref[p, group] = white[group * rows : group * rows + share]
            own_ref[p, group] = white[group * rows + share : (group + 1) * rows].astype(F32) * scale


def gather_lags(ends, re, im):
    half = PH // 2
    quarter = half // 2
    both = [None] + [re[p] + re[half - p] for p in range(1, quarter)]
    apart = [None] + [re[p] - re[half - p] for p in range(1, quarter)]
    oboth = [None] + [im[p] + im[half - p] for p in range(1, quarter)]
    oapart = [None] + [im[p] - im[half - p] for p in range(1, quarter)]
    edge = (ends[0] + ends[1], ends[0] - ends[1])
    cosines, sines = {}, {}
    for n in range(NN // 2 + 1):
        fold, total = (both, edge[0]) if n % 2 == 0 else (apart, edge[1])
        if n % 2 == 0:
            total = total + re[quarter] if (n // 2) % 2 == 0 else total - re[quarter]
        for p in range(1, quarter):
            c = math.cos(2 * math.pi * p * n / PH)
            if abs(abs(c) - 1) < 1e-9:
                total = total + fold[p] if c > 0 else total - fold[p]
            elif abs(c) > 1e-9:
                total = total + fold[p] * c
        cosines[n] = total
        if n:
            ofold = oapart if n % 2 == 0 else oboth
            total = None
            for p in range(1, quarter):
                s = math.sin(2 * math.pi * p * n / PH)
                if abs(s) > 1e-9:
                    term = ofold[p] if abs(s - 1) < 1e-9 else -ofold[p] if abs(s + 1) < 1e-9 else ofold[p] * s
                    total = term if total is None else total + term
            if n % 2:
                total = total + im[quarter] if n % 4 == 1 else total - im[quarter]
            sines[n] = total
    lags = []
    for n in range(-NN // 2, NN // 2):
        if n == 0:
            lags.append(cosines[0])
        else:
            lags.append(cosines[-n] + sines[-n] if n < 0 else cosines[n] - sines[n])
    return lags


def pair_kernel(mine, own_ref, src_ref, table_ref, turn_ref, *refs):
    out_hbm, wide_ref, pair_a, pair_b, lag_a, lag_b, out_ref, sems = refs[-8:]
    groups, chans = own_ref.shape[1:3]
    share = src_ref.shape[2]
    wide_ref[...] = src_ref[...].astype(F32)
    size = GROUP * chans
    core = lax.axis_index("file") % 2
    place = (core if mine else 1 - core) * share

    def written(i):
        return pltpu.make_async_copy(
            out_ref.at[pl.ds(i * GROUP, GROUP)],
            out_hbm.at[pl.ds(place + i * GROUP, GROUP)],
            sems.at[i],
        )

    def cross(first, pair_ref):
        for p in range(PAIRS):
            for part in range(2):
                left = 2 * NA * part
                own = [
                    (own_ref[p, g, :, left : left + NA], own_ref[p, g, :, left + NA : left + 2 * NA])
                    for g in range(groups)
                ]
                for s in range(0, GROUP, 2):
                    res, ims = [], []
                    for one in range(2):
                        cre, cim = None, None
                        for g in range(groups):
                            at = first + s + one
                            sre = wide_ref[p, g, at : at + 1, left : left + NA]
                            sim = wide_ref[p, g, at : at + 1, left + NA : left + 2 * NA]
                            ore, oim = own[g]
                            tre = ore * sre + oim * sim
                            tim = oim * sre - ore * sim
                            cre = tre if cre is None else cre + tre
                            cim = tim if cim is None else cim + tim
                        res.append(cre)
                        ims.append(cim)
                    at = slice(s * chans, (s + 2) * chans)
                    pair_ref[p, at, left : left + NA] = jnp.concatenate(res, 0).astype(BF16)
                    pair_ref[p, at, left + NA : left + 2 * NA] = jnp.concatenate(ims, 0).astype(BF16)

    def product(pair_ref, lag_ref):
        lag_ref[0] = jnp.dot(pair_ref[0], table_ref[0], preferred_element_type=F32)
        lag_ref[1:] = jnp.dot(
            pair_ref[1:].reshape((PAIRS - 1) * size, 4 * NA),
            table_ref[1],
            preferred_element_type=F32,
        ).reshape(PAIRS - 1, size, 2 * LO)

    def lags(first, lag_ref):
        for s in range(GROUP):
            at = slice(s * chans, (s + 1) * chans)
            for h in range(HALF):
                lo = 128 * h
                ends = [lag_ref[0, at, LO * i + lo : LO * i + lo + 128] for i in range(2)]
                re, im = [None], [None]
                for p in range(1, PAIRS):
                    u = lag_ref[p, at, lo : lo + 128]
                    v = lag_ref[p, at, LO + lo : LO + lo + 128]
                    c = turn_ref[0, p, :, lo : lo + 128]
                    d = turn_ref[1, p, :, lo : lo + 128]
                    re.append(c * u - d * v)
                    im.append(c * v + d * u)
                for n, value in enumerate(gather_lags(ends, re, im)):
                    out_ref[first + s, :, LO * n + lo : LO * n + lo + 128] = value

    steps = share // GROUP
    pairs, lagged = (pair_a, pair_b), (lag_a, lag_b)
    cross(0, pair_a)
    for i in range(steps):
        product(pairs[i % 2], lagged[i % 2])
        if i + 1 < steps:
            cross((i + 1) * GROUP, pairs[(i + 1) % 2])
        if i:
            lags((i - 1) * GROUP, lagged[(i - 1) % 2])
            written(i - 1).start()
    lags((steps - 1) * GROUP, lagged[(steps - 1) % 2])
    written(steps - 1).start()
    for i in range(steps):
        written(i).wait()


def pair_call(mine, own, src, table, turn, sources, done=None):
    groups, chans = own.shape[1:3]
    share = src.shape[2]
    vmem = pl.BlockSpec(memory_space=pltpu.VMEM)
    hbm = pl.BlockSpec(memory_space=pltpu.HBM)
    operands = [own, src, table, turn]
    specs = [vmem] * 4
    aliases = {}
    if done is not None:
        aliases = {len(operands): 0}
        operands.append(done)
        specs.append(hbm)
    return pl.pallas_call(
        functools.partial(pair_kernel, mine),
        in_specs=specs,
        out_specs=hbm,
        scratch_shapes=[
            pltpu.VMEM((PAIRS, groups, share, 4 * NA), F32),
            pltpu.VMEM((PAIRS, GROUP * chans, 4 * NA), BF16),
            pltpu.VMEM((PAIRS, GROUP * chans, 4 * NA), BF16),
            pltpu.VMEM((PAIRS, GROUP * chans, 2 * LO), F32),
            pltpu.VMEM((PAIRS, GROUP * chans, 2 * LO), F32),
            pltpu.VMEM((share, chans, SEG), F32),
            pltpu.SemaphoreType.DMA((share // GROUP,)),
        ],
        out_shape=jax.ShapeDtypeStruct((sources, chans, SEG), F32),
        input_output_aliases=aliases,
        compiler_params=pltpu.CompilerParams(vmem_limit_bytes=32 * 2**20),
        name="pair",
    )(*operands)


def local(raw, fir_taps, offsets, vs_index):
    samples = raw[0]
    channels = samples.shape[0]
    files = lax.axis_size("file")
    wins = lax.axis_size("win")
    sources = vs_index.shape[0] // wins
    share = sources // 2
    chans = channels // files
    rows = share + chans
    segs = files * TD // SEG
    groups = wins * segs
    taps = fir_taps[None, :]
    index = vs_index[None, :]
    table = transform_table()
    scale = 1.0 / math.sqrt(SEG * segs * wins)
    hbm = pl.BlockSpec(memory_space=pltpu.HBM)
    vmem = pl.BlockSpec(memory_space=pltpu.VMEM)
    packed = pl.pallas_call(
        functools.partial(decimate_kernel, files, wins),
        out_shape=jax.ShapeDtypeStruct((files * wins, 2 * chans + rows, TD), BF16),
        in_specs=[hbm] * 4,
        out_specs=vmem,
        scratch_shapes=[
            pltpu.SMEM(offsets.shape, jnp.int32),
            pltpu.VMEM(taps.shape, F32),
            pltpu.VMEM(index.shape, jnp.int32),
            pltpu.VMEM(samples.shape, BF16),
            pltpu.SemaphoreType.DMA((4,)),
        ],
        compiler_params=pltpu.CompilerParams(vmem_limit_bytes=60 * 2**20),
        name="decimate",
    )(offsets, taps, index, samples)
    data = lax.all_to_all(packed, ("file", "win"), split_axis=0, concat_axis=0, tiled=True)
    own, src, table_high, turn = pl.pallas_call(
        functools.partial(forward_kernel, files, wins, chans, scale),
        out_shape=(
            jax.ShapeDtypeStruct((PAIRS, groups, chans, 4 * NA), F32),
            jax.ShapeDtypeStruct((PAIRS, groups, share, 4 * NA), BF16),
            jax.ShapeDtypeStruct(table.shape[1:], BF16),
            jax.ShapeDtypeStruct((2, PAIRS, 8, LO), F32),
        ),
        in_specs=[vmem, hbm],
        out_specs=(vmem, vmem, vmem, vmem),
        scratch_shapes=[
            pltpu.VMEM(table.shape[1:], BF16),
            pltpu.VMEM((files * wins, rows, TD), F32),
            pltpu.VMEM((PAIRS, groups * rows, 2 * LO), BF16),
            pltpu.VMEM((PAIRS, groups * rows, 2 * LO), BF16),
            pltpu.VMEM((PAIRS, groups * rows, 4 * NA), F32),
            pltpu.SemaphoreType.DMA((2,)),
        ],
        compiler_params=pltpu.CompilerParams(vmem_limit_bytes=103 * 2**19),
        name="forward",
    )(data, table)
    other = lax.ppermute(src, "file", [(i, i ^ 1) for i in range(files)])
    half = pair_call(True, own, src, table_high, turn, sources)
    return pair_call(False, own, other, table_high, turn, sources, half)


def solution(mesh):
    return jax.shard_map(
        local,
        mesh=mesh,
        in_specs=(P("win", None, "file"), P(), P("win", "file"), P()),
        out_specs=P("win", "file", None),
        check_vma=False,
    )
```

time: 40.8 us -> 30.4 us (0.75)
  Pallas kernels: 13.3 us -> 9.97 us
  local copies, waits for them, and re-layouts: 3.04 us -> 0 us
  blocking collectives: 21 us -> 19 us
  starting transfers between devices: 2.35 us -> 0.46 us
    pallas_call x1 -> x3, Pallas kernels: 12.3 us -> 7.4 us  [the longest x2 4.39 us: pair_call(): pl.pallas_call(functools.partial(pair_kernel, mine), in_specs=specs, out_...]
    unnamed x6 -> x0, local copies, waits for them, and re-layouts: 2.28 us -> none
    all_to_all x1, blocking collectives: 21 us -> 19 us  [local(): lax.all_to_all(packed, ('file', 'win'), split_axis=0, concat_axis=0, tile...]
    ppermute x1, starting transfers between devices: 2.35 us -> 0.46 us  [local(): other = lax.ppermute(src, 'file', [(i, i ^ 1) for i in range(files)])]
    pallas_call x1, Pallas kernels: 1.03 us -> 2.57 us  [local(): pl.pallas_call(functools.partial(decimate_kernel, files, wins), out_shape...]
    slice x1 -> x0, local copies, waits for them, and re-layouts: 0.76 us -> none  [local(): samples[:, samples.shape[1] - 128:]]
  transfers between devices with their start and end apart: 1 -> 1, of which waited for: 1 -> 0; matrix products, arithmetic and copies ran while one was open for 0% -> 0% of each run, Pallas kernels for 0% -> 7%
where the time goes in v2:
time: 30.4 us; the launch traced here: 30.2 us
  blocking collectives  19 us (62%)
  Pallas kernels  9.97 us (33%)
  between operations  0.68 us (2%)
  starting transfers between devices  0.46 us (2%)
    all_to_all x1, blocking collectives, local(): lax.all_to_all(packed, ('file', 'win'), split_axis=0, concat_axis=0, tile...  19 us
    pallas_call x2, Pallas kernels, pair_call(): pl.pallas_call(functools.partial(pair_kernel, mine), in_specs=specs, out_...  4.39 us
    pallas_call x1, Pallas kernels, local(): pl.pallas_call(functools.partial(forward_kernel, files, wins, chans, scal...  3.01 us
    pallas_call x1, Pallas kernels, local(): pl.pallas_call(functools.partial(decimate_kernel, files, wins), out_shape...  2.57 us
  transfers between devices with their start and end apart: 1, of which 0 were waited for; matrix products, arithmetic and copies ran while one was open for 0% of the time, Pallas kernels for 7%

profile of v2, /device:TPU:0, one launch (start us, length us, event | category | flops | bytes accessed | tf_op | source)
XLA Modules:
  0.0 30.2 jit_solution(11087089600371307473)
XLA Ops:
  0.7 2.6 %decimate.1 = bf16[32,40,128]{2,1,0:T(8,128)(2,1)} custom-call(s32[1,1]{1,0:T(1,128)S(6)} %copy.8.offset_hbm, f32[1,64]{1,0:T(1,128)} %bitcast.4, s32[1,64]{1,0:T(1,128)} %bitcast.5, bf16[128,1280]{1,0:T(8,128)(2,1)} %bitcast.3), custom_call_target="tpu_custom_call" | custom-call | tf_op jit(solution)/shard_map/decimate/pallas_call | solution.py:489
  3.2 19.0 %all_to_all.5.data_ref = bf16[32,40,128]{2,1,0:T(8,128)(2,1)S(1)} all-to-all(bf16[32,40,128]{2,1,0:T(8,128)(2,1)} %decimate.1), channel_id=1, replica_groups=mesh['file'=16,'win'=2] {'file','win'}, dimensions={0} | all-to-all | bytes 655360 | tf_op jit(solution)/shard_map/all_to_all | solution.py:504
  22.3 3.0 %forward.1 = (f32[8,2,8,512]{3,2,1,0:T(8,128)S(1)}, bf16[8,2,16,512]{3,2,1,0:T(8,128)(2,1)S(1)}, bf16[2,512,512]{2,1,0:T(8,128)(2,1)S(1)}, f32[2,8,8,256]{3,2,1,0:T(8,128)S(1)}) custom-call(bf16[32,40,128]{2,1,0:T(8,128)(2,1)S(1)} %all_to_all.5.data_ref, bf16[2,2,512,512]{3,2,1,0:T(8,128)(2,1)} %constant.2.clone.table_hbm), custom_call_target="tpu_custom_call" | custom-call | tf_op jit(solution)/shard_map/forward/pallas_call | solution.py:505
  25.3 0.5 %collective-permute-start = (bf16[8,2,16,512]{3,2,1,0:T(8,128)(2,1)S(1)}, bf16[8,2,16,512]{3,2,1,0:T(8,128)(2,1)S(1)}, u32[]{:S(2)}, u32[]{:S(2)}) collective-permute-start(bf16[8,2,16,512]{3,2,1,0:T(8,128)(2,1)S(1)} %get-tuple-element.10.src_ref), channel_id=1, source_target_pairs={{0,2},{2,0},{4,6},{6,4},{8,10},{10,8},{12,14},{14,12},{16,18},{18,... | collective-permute-start | bytes 786440 | tf_op jit(solution)/shard_map/ppermute | solution.py:526
  25.7 2.2 %pair.2.refs_0_ = f32[32,8,2048]{2,1,0:T(8,128)} custom-call(f32[8,2,8,512]{3,2,1,0:T(8,128)S(1)} %get-tuple-element.9.own_ref, bf16[8,2,16,512]{3,2,1,0:T(8,128)(2,1)S(1)} %get-tuple-element.10.src_ref, bf16[2,512,512]{2,1,0:T(8,128)(2,1)S(1)} %get-tuple-element.11.table_ref, f32[2,8,8,256]{3,2,1,0:T(8,128)S(1)} %get-tuple-element.12.turn_ref), custom_call_target="tpu_custom_call" | custom-call | tf_op jit(solution)/shard_map/pair/pallas_call | solution.py:452
  27.9 0.0 collective-permute-done.src_ref
  28.0 2.2 %pair.3 = f32[32,8,2048]{2,1,0:T(8,128)} custom-call(f32[8,2,8,512]{3,2,1,0:T(8,128)S(1)} %get-tuple-element.9.own_ref, bf16[8,2,16,512]{3,2,1,0:T(8,128)(2,1)S(1)} %collective-permute-done.src_ref, bf16[2,512,512]{2,1,0:T(8,128)(2,1)S(1)} %get-tuple-element.11.table_ref, ...), custom_call_target="tpu_custom_call", output_to_operand_aliasing={{}: (4, {})} | custom-call | tf_op jit(solution)/shard_map/pair/pallas_call | solution.py:452
Async XLA Ops:
  25.3 2.7 %collective-permute-start = (bf16[8,2,16,512]{3,2,1,0:T(8,128)(2,1)S(1)}, bf16[8,2,16,512]{3,2,1,0:T(8,128)(2,1)S(1)}, u32[]{:S(2)}, u32[]{:S(2)}) collective-permute-start(bf16[8,2,16,512]{3,2,1,0:T(8,128)(2,1)S(1)} %get-tuple-element.10.src_ref), channel_id=1, source_target_pairs={{0,2},{2,0},{4,6},{6,4},{8,10},{10,8},{12,14},{14,12},{16,18},{18,... | collective-permute-start | bytes 786440 | tf_op jit(solution)/shard_map/ppermute | solution.py:526

commit v3 on v2

--- a/solution.py
+++ b/solution.py
@@ -23,17 +23,13 @@
 HALF = LO // 128
 PAIRS = PH // 2
 EARLY = 8
-GROUP = 4
+GROUPS = (8, 4)
+TABLE_ROWS = 2048
 
 NT = (((1,), (1,)), ((), ()))
 NN_DIMS = (((1,), (0,)), ((), ()))
 F32 = jnp.float32
 BF16 = jnp.bfloat16
-
-
-def split_table(x):
-    high = x.astype(BF16)
-    return np.stack([high, (x - high.astype(np.float64)).astype(BF16)])
 
 
 def transform_table():
@@ -50,7 +46,13 @@
     c8, s8 = wave(PH * a + PH // 2)
     z = np.zeros_like(c)
     ends = np.block([[c, z], [-s, z], [z, c8], [z, -s8]])
-    return jnp.asarray(split_table(np.stack([ends, folded])))
+    waves = np.concatenate([c, s, cc, ss, c8, s8])
+    high = waves.astype(BF16)
+    low = (waves - high.astype(np.float64)).astype(BF16)
+    inverse = np.concatenate([ends, folded]).astype(BF16)
+    parts = [inverse, np.concatenate([high, low], axis=1)]
+    spare = TABLE_ROWS - sum(len(part) for part in parts)
+    return jnp.asarray(np.concatenate(parts + [np.zeros((spare, 2 * LO), BF16)]))
 
 
 def three_pass(high, low, table_high, table_low, dims):
@@ -93,15 +95,13 @@
     lane = lax.broadcasted_iota(jnp.int32, (TAPS, 256), 1)
     place = jnp.where(lane == 128 - k, 1.0, 0.0).astype(BF16)
     band = jnp.dot(taps, place, preferred_element_type=F32)
-    shift = lax.broadcasted_iota(jnp.int32, (half, 128), 0) * R + offset
-    wide_shift = jnp.concatenate([shift, shift], axis=1)
-    for bit in range(7):
-        band = jnp.where((wide_shift >> bit) % 2 == 1, pltpu.roll(band, 1 << bit, 1), band)
-    tiles = []
-    for t in range(width // 128):
-        low = jnp.where(shift // 128 == t, band[:, :128], 0.0)
-        tiles.append(low + jnp.where(shift // 128 == t - 1, band[:, 128:], 0.0))
-    rolled = jnp.concatenate(tiles, axis=1).astype(BF16)
+    band = pltpu.roll(band[:8], offset, 1)
+    row = lax.broadcasted_iota(jnp.int32, (8, 256), 0)
+    for bit in range(3):
+        band = jnp.where((row >> bit) % 2 == 1, pltpu.roll(band, R << bit, 1), band)
+    band = jnp.concatenate([band, jnp.zeros((8, width - 256), F32)], axis=1)
+    tiles = [band if not i else pltpu.roll(band, 8 * R * i, 1) for i in range(half // 8)]
+    rolled = jnp.concatenate(tiles, axis=0).astype(BF16)
     zero = jnp.zeros((half, width), BF16)
     first = jnp.concatenate([rolled, zero], axis=0)
     second = jnp.concatenate([zero, rolled], axis=0)
@@ -183,16 +183,18 @@
 def forward_kernel(
     files, wins, chans, scale,
     data_ref, table_hbm, own_ref, src_ref, table_ref, turn_ref,
-    rest_ref, fixed_ref, high_ref, low_ref, spec_ref, sems,
+    waves_ref, fixed_ref, high_ref, low_ref, spec_ref, sems,
 ):
     copies = [
         pltpu.make_async_copy(source, target, sems.at[i])
         for i, (source, target) in enumerate(
-            ((table_hbm.at[0], table_ref), (table_hbm.at[1], rest_ref))
+            (
+                (table_hbm.at[pl.ds(8 * NA, 6 * NA)], waves_ref),
+                (table_hbm.at[pl.ds(0, 8 * NA)], table_ref),
+            )
         )
     ]
-    for copy in copies:
-        copy.start()
+    copies[0].start()
     phase = lax.broadcasted_iota(jnp.int32, (8, LO), 0) * lax.broadcasted_iota(jnp.int32, (8, LO), 1)
     angle = phase.astype(F32) * (math.pi / SEG)
     turns = (jnp.cos(angle), jnp.sin(angle))
@@ -271,22 +273,36 @@
                     else:
                         re, im = terms[0][0], terms[PAIRS][0]
                     for part, value in enumerate((re, im)):
-                        at = slice(LO * part + 128 * h, LO * part + 128 * h + 128)
+                        at = slice(128 * h, 128 * h + 128)
                         high, low = split(value)
-                        high_ref[p, base : base + rows, at] = high
-                        low_ref[p, base : base + rows, at] = low
+                        high_ref[part, p, base : base + rows, at] = high
+                        low_ref[part, p, base : base + rows, at] = low
     groups = wins * segs
     count = groups * rows
-    for copy in copies:
-        copy.wait()
-    spec_ref[0] = three_pass(high_ref[0], low_ref[0], table_ref[0], rest_ref[0], NT)
-    spec_ref[1:] = three_pass(
-        high_ref[1:].reshape((PAIRS - 1) * count, 2 * LO),
-        low_ref[1:].reshape((PAIRS - 1) * count, 2 * LO),
-        table_ref[1],
-        rest_ref[1],
-        NT,
-    ).reshape(PAIRS - 1, count, 4 * NA)
+    copies[0].wait()
+    copies[1].start()
+
+    def product(part, first, last, begin, end):
+        lines = (last - first) * count
+        return three_pass(
+            high_ref[part, first:last].reshape(lines, LO),
+            low_ref[part, first:last].reshape(lines, LO),
+            waves_ref[begin * NA : end * NA, :LO],
+            waves_ref[begin * NA : end * NA, LO:],
+            NT,
+        ).reshape(last - first, count, (end - begin) * NA)
+
+    for part, begin in enumerate((0, 4)):
+        value = product(part, 0, 1, begin, begin + 2)[0]
+        spec_ref[0, :, 2 * NA * part : 2 * NA * part + NA] = value[:, :NA]
+        spec_ref[0, :, 2 * NA * part + NA : 2 * NA * (part + 1)] = -value[:, NA:]
+    of_re = product(0, 1, PAIRS, 0, 4)
+    of_im = product(1, 1, PAIRS, 0, 4)
+    c, s, cc, ss = (slice(NA * i, NA * (i + 1)) for i in range(4))
+    spec_ref[1:, :, c] = of_re[..., c] + of_im[..., s]
+    spec_ref[1:, :, s] = of_im[..., c] - of_re[..., s]
+    spec_ref[1:, :, cc] = of_re[..., cc] - of_im[..., ss]
+    spec_ref[1:, :, ss] = -(of_im[..., cc] + of_re[..., ss])
     total = jnp.zeros((count, NA), F32)
     for p in range(PAIRS):
         for part in range(2):
@@ -300,17 +316,23 @@
     per_band = BAND // PH
     band = jnp.where(row // per_band == lane // per_band, 1.0, 0.0).astype(BF16)
     amplitude = (
-        jnp.dot(high, band, preferred_element_type=F32)
-        + jnp.dot(low, band, preferred_element_type=F32)
-        + jnp.dot(low2, band, preferred_element_type=F32)
-    ) * (1.0 / BAND) + EPSILON
+        jnp.dot(
+            jnp.concatenate([high, low, low2], axis=1),
+            jnp.concatenate([band] * 3, axis=0),
+            preferred_element_type=F32,
+        )
+        * (1.0 / BAND)
+        + EPSILON
+    )
     gain = 1.0 / amplitude
     gain = jnp.concatenate([gain] * 4, axis=1)
-    for p in range(PAIRS):
-        white = (spec_ref[p] * gain).astype(BF16)
-        for group in range(groups):
-            src_ref[p, group] = white[group * rows : group * rows + share]
-            own_ref[p, group] = white[group * rows + share : (group + 1) * rows].astype(F32) * scale
+    for group in range(groups):
+        at = slice(group * rows, group * rows + share)
+        own = slice(group * rows + share, (group + 1) * rows)
+        for p in range(PAIRS):
+            src_ref[p, group] = (spec_ref[p, at] * gain[at]).astype(BF16)
+            own_ref[p, group] = (spec_ref[p, own] * gain[own]).astype(BF16).astype(F32) * scale
+    copies[1].wait()
 
 
 def gather_lags(ends, re, im):
@@ -353,21 +375,32 @@
     return lags
 
 
-def pair_kernel(mine, own_ref, src_ref, table_ref, turn_ref, *refs):
-    out_hbm, wide_ref, pair_a, pair_b, lag_a, lag_b, out_ref, sems = refs[-8:]
+def pair_kernel(last, group_size, own_ref, src_ref, table_ref, turn_ref, *refs):
+    if last:
+        done_ref, out_hbm, wide_ref, pair_a, pair_b, lag_a, lag_b, out_ref, sems = refs
+    else:
+        out_ref, wide_ref, pair_a, pair_b, lag_a, lag_b = refs
     groups, chans = own_ref.shape[1:3]
     share = src_ref.shape[2]
+    size = group_size * chans
+    copies = []
+
+    def write(source, place, count):
+        if last:
+            copies.append(
+                pltpu.make_async_copy(source, out_hbm.at[pl.ds(place, count)], sems.at[len(copies)])
+            )
+            copies[-1].start()
+
+    if last:
+        core = lax.axis_index("file") % 2
+        write(done_ref, core * share, share)
+        place = (1 - core) * share
     wide_ref[...] = src_ref[...].astype(F32)
-    size = GROUP * chans
-    core = lax.axis_index("file") % 2
-    place = (core if mine else 1 - core) * share
-
-    def written(i):
-        return pltpu.make_async_copy(
-            out_ref.at[pl.ds(i * GROUP, GROUP)],
-            out_hbm.at[pl.ds(place + i * GROUP, GROUP)],
-            sems.at[i],
-        )
+
+    def finished(first):
+        if last:
+            write(out_ref.at[pl.ds(first, group_size)], place + first, group_size)
 
     def cross(first, pair_ref):
         for p in range(PAIRS):
@@ -377,7 +410,7 @@
                     (own_ref[p, g, :, left : left + NA], own_ref[p, g, :, left + NA : left + 2 * NA])
                     for g in range(groups)
                 ]
-                for s in range(0, GROUP, 2):
+                for s in range(0, group_size, 2):
                     res, ims = [], []
                     for one in range(2):
                         cre, cim = None, None
@@ -397,15 +430,15 @@
                     pair_ref[p, at, left + NA : left + 2 * NA] = jnp.concatenate(ims, 0).astype(BF16)
 
     def product(pair_ref, lag_ref):
-        lag_ref[0] = jnp.dot(pair_ref[0], table_ref[0], preferred_element_type=F32)
+        lag_ref[0] = jnp.dot(pair_ref[0], table_ref[: 4 * NA], preferred_element_type=F32)
         lag_ref[1:] = jnp.dot(
             pair_ref[1:].reshape((PAIRS - 1) * size, 4 * NA),
-            table_ref[1],
+            table_ref[4 * NA :],
             preferred_element_type=F32,
         ).reshape(PAIRS - 1, size, 2 * LO)
 
     def lags(first, lag_ref):
-        for s in range(GROUP):
+        for s in range(group_size):
             at = slice(s * chans, (s + 1) * chans)
             for h in range(HALF):
                 lo = 128 * h
@@ -421,51 +454,46 @@
                 for n, value in enumerate(gather_lags(ends, re, im)):
                     out_ref[first + s, :, LO * n + lo : LO * n + lo + 128] = value
 
-    steps = share // GROUP
+    steps = share // group_size
     pairs, lagged = (pair_a, pair_b), (lag_a, lag_b)
     cross(0, pair_a)
     for i in range(steps):
         product(pairs[i % 2], lagged[i % 2])
         if i + 1 < steps:
-            cross((i + 1) * GROUP, pairs[(i + 1) % 2])
+            cross((i + 1) * group_size, pairs[(i + 1) % 2])
         if i:
-            lags((i - 1) * GROUP, lagged[(i - 1) % 2])
-            written(i - 1).start()
-    lags((steps - 1) * GROUP, lagged[(steps - 1) % 2])
-    written(steps - 1).start()
-    for i in range(steps):
-        written(i).wait()
-
-
-def pair_call(mine, own, src, table, turn, sources, done=None):
+            lags((i - 1) * group_size, lagged[(i - 1) % 2])
+            finished((i - 1) * group_size)
+    lags((steps - 1) * group_size, lagged[(steps - 1) % 2])
+    finished((steps - 1) * group_size)
+    for copy in copies:
+        copy.wait()
+
+
+def pair_call(own, src, table, turn, done=None):
     groups, chans = own.shape[1:3]
     share = src.shape[2]
     vmem = pl.BlockSpec(memory_space=pltpu.VMEM)
     hbm = pl.BlockSpec(memory_space=pltpu.HBM)
-    operands = [own, src, table, turn]
-    specs = [vmem] * 4
-    aliases = {}
-    if done is not None:
-        aliases = {len(operands): 0}
-        operands.append(done)
-        specs.append(hbm)
+    last = done is not None
+    group_size = min(GROUPS[last], share)
+    operands = [own, src, table, turn] + [done] * last
+    scratch = [pltpu.VMEM((PAIRS, groups, share, 4 * NA), F32)]
+    scratch += [pltpu.VMEM((PAIRS, group_size * chans, 4 * NA), BF16)] * 2
+    scratch += [pltpu.VMEM((PAIRS, group_size * chans, 2 * LO), F32)] * 2
+    if last:
+        scratch += [
+            pltpu.VMEM((share, chans, SEG), F32),
+            pltpu.SemaphoreType.DMA((1 + share // group_size,)),
+        ]
     return pl.pallas_call(
-        functools.partial(pair_kernel, mine),
-        in_specs=specs,
-        out_specs=hbm,
-        scratch_shapes=[
-            pltpu.VMEM((PAIRS, groups, share, 4 * NA), F32),
-            pltpu.VMEM((PAIRS, GROUP * chans, 4 * NA), BF16),
-            pltpu.VMEM((PAIRS, GROUP * chans, 4 * NA), BF16),
-            pltpu.VMEM((PAIRS, GROUP * chans, 2 * LO), F32),
-            pltpu.VMEM((PAIRS, GROUP * chans, 2 * LO), F32),
-            pltpu.VMEM((share, chans, SEG), F32),
-            pltpu.SemaphoreType.DMA((share // GROUP,)),
-        ],
-        out_shape=jax.ShapeDtypeStruct((sources, chans, SEG), F32),
-        input_output_aliases=aliases,
+        functools.partial(pair_kernel, last, group_size),
+        in_specs=[vmem] * len(operands),
+        out_specs=hbm if last else vmem,
+        scratch_shapes=scratch,
+        out_shape=jax.ShapeDtypeStruct((share * (2 if last else 1), chans, SEG), F32),
         compiler_params=pltpu.CompilerParams(vmem_limit_bytes=32 * 2**20),
-        name="pair",
+        name="pair_last" if last else "pair_first",
     )(*operands)
 
 
@@ -507,16 +535,16 @@
         out_shape=(
             jax.ShapeDtypeStruct((PAIRS, groups, chans, 4 * NA), F32),
             jax.ShapeDtypeStruct((PAIRS, groups, share, 4 * NA), BF16),
-            jax.ShapeDtypeStruct(table.shape[1:], BF16),
+            jax.ShapeDtypeStruct((8 * NA, 2 * LO), BF16),
             jax.ShapeDtypeStruct((2, PAIRS, 8, LO), F32),
         ),
         in_specs=[vmem, hbm],
         out_specs=(vmem, vmem, vmem, vmem),
         scratch_shapes=[
-            pltpu.VMEM(table.shape[1:], BF16),
+            pltpu.VMEM((6 * NA, 2 * LO), BF16),
             pltpu.VMEM((files * wins, rows, TD), F32),
-            pltpu.VMEM((PAIRS, groups * rows, 2 * LO), BF16),
-            pltpu.VMEM((PAIRS, groups * rows, 2 * LO), BF16),
+            pltpu.VMEM((2, PAIRS, groups * rows, LO), BF16),
+            pltpu.VMEM((2, PAIRS, groups * rows, LO), BF16),
             pltpu.VMEM((PAIRS, groups * rows, 4 * NA), F32),
             pltpu.SemaphoreType.DMA((2,)),
         ],
@@ -524,8 +552,8 @@
         name="forward",
     )(data, table)
     other = lax.ppermute(src, "file", [(i, i ^ 1) for i in range(files)])
-    half = pair_call(True, own, src, table_high, turn, sources)
-    return pair_call(False, own, other, table_high, turn, sources, half)
+    half = pair_call(own, src, table_high, turn)
+    return pair_call(own, other, table_high, turn, half)
 
 
 def solution(mesh):

time: 30.4 us -> 28.9 us (0.951)
  Pallas kernels: 9.97 us -> 8.52 us
    pallas_call x2, Pallas kernels: 4.39 us -> 3.39 us  [pair_call(): pl.pallas_call(functools.partial(pair_kernel, last, group_size), in_specs...]
  transfers between devices with their start and end apart: 1 -> 1, of which waited for: 0 -> 0; matrix products, arithmetic and copies ran while one was open for 0% -> 0% of each run, Pallas kernels for 7% -> 4%
where the time goes in v3:
time: 28.9 us; the launch traced here: 28.7 us
  blocking collectives  19 us (66%)
  Pallas kernels  8.52 us (29%)
  between operations  0.68 us (2%)
  starting transfers between devices  0.45 us (2%)
    all_to_all x1, blocking collectives, local(): lax.all_to_all(packed, ('file', 'win'), split_axis=0, concat_axis=0, tile...  19 us
    pallas_call x2, Pallas kernels, pair_call(): pl.pallas_call(functools.partial(pair_kernel, last, group_size), in_specs...  3.39 us
    pallas_call x1, Pallas kernels, local(): pl.pallas_call(functools.partial(forward_kernel, files, wins, chans, scal...  2.71 us
    pallas_call x1, Pallas kernels, local(): pl.pallas_call(functools.partial(decimate_kernel, files, wins), out_shape...  2.42 us
  transfers between devices with their start and end apart: 1, of which 0 were waited for; matrix products, arithmetic and copies ran while one was open for 0% of the time, Pallas kernels for 4%

profile of v3, /device:TPU:0, one launch (start us, length us, event | category | flops | bytes accessed | tf_op | source)
XLA Modules:
  0.0 28.7 jit_solution(12788286915345346448)
XLA Ops:
  0.7 2.4 %decimate.1 = bf16[32,40,128]{2,1,0:T(8,128)(2,1)} custom-call(s32[1,1]{1,0:T(1,128)S(6)} %copy.6.offset_hbm, f32[1,64]{1,0:T(1,128)} %bitcast.4, s32[1,64]{1,0:T(1,128)} %bitcast.5, bf16[128,1280]{1,0:T(8,128)(2,1)} %bitcast.3), custom_call_target="tpu_custom_call" | custom-call | tf_op jit(solution)/shard_map/decimate/pallas_call | solution.py:517
  3.1 19.0 %all_to_all.5.data_ref = bf16[32,40,128]{2,1,0:T(8,128)(2,1)S(1)} all-to-all(bf16[32,40,128]{2,1,0:T(8,128)(2,1)} %decimate.1), channel_id=1, replica_groups=mesh['file'=16,'win'=2] {'file','win'}, dimensions={0} | all-to-all | bytes 655360 | tf_op jit(solution)/shard_map/all_to_all | solution.py:532
  22.1 2.7 %forward.1 = (f32[8,2,8,512]{3,2,1,0:T(8,128)S(1)}, bf16[8,2,16,512]{3,2,1,0:T(8,128)(2,1)S(1)}, bf16[1024,512]{1,0:T(8,128)(2,1)S(1)}, f32[2,8,8,256]{3,2,1,0:T(8,128)S(1)}) custom-call(bf16[32,40,128]{2,1,0:T(8,128)(2,1)S(1)} %all_to_all.5.data_ref, bf16[2048,512]{1,0:T(8,128)(2,1)} %constant.2.clone.table_hbm), custom_call_target="tpu_custom_call" | custom-call | tf_op jit(solution)/shard_map/forward/pallas_call | solution.py:533
  24.8 0.5 %collective-permute-start = (bf16[8,2,16,512]{3,2,1,0:T(8,128)(2,1)S(1)}, bf16[8,2,16,512]{3,2,1,0:T(8,128)(2,1)S(1)}, u32[]{:S(2)}, u32[]{:S(2)}) collective-permute-start(bf16[8,2,16,512]{3,2,1,0:T(8,128)(2,1)S(1)} %get-tuple-element.10.src_ref), channel_id=1, source_target_pairs={{0,2},{2,0},{4,6},{6,4},{8,10},{10,8},{12,14},{14,12},{16,18},{18,... | collective-permute-start | bytes 786440 | tf_op jit(solution)/shard_map/ppermute | solution.py:554
  25.3 1.2 %pair_first.1.refs_0_ = f32[16,8,2048]{2,1,0:T(8,128)S(1)} custom-call(f32[8,2,8,512]{3,2,1,0:T(8,128)S(1)} %get-tuple-element.9.own_ref, bf16[8,2,16,512]{3,2,1,0:T(8,128)(2,1)S(1)} %get-tuple-element.10.src_ref, bf16[1024,512]{1,0:T(8,128)(2,1)S(1)} %get-tuple-element.11.table_ref, f32[2,8,8,256]{3,2,1,0:T(8,128)S(1)} %get-tuple-element.12.turn_ref), custom_call_target="tpu_custom_call" | custom-call | tf_op jit(solution)/shard_map/pair_first/pallas_call | solution.py:489
  26.5 0.0 collective-permute-done.src_ref
  26.5 2.2 %pair_last.1 = f32[32,8,2048]{2,1,0:T(8,128)} custom-call(f32[8,2,8,512]{3,2,1,0:T(8,128)S(1)} %get-tuple-element.9.own_ref, bf16[8,2,16,512]{3,2,1,0:T(8,128)(2,1)S(1)} %collective-permute-done.src_ref, bf16[1024,512]{1,0:T(8,128)(2,1)S(1)} %get-tuple-element.11.table_ref, f32[2,8,8,256]{3,2,1,0:T(8,128)S(1)} %get-tuple-element.12.turn_ref, ...), custom_call_target="tpu_custom_call" | custom-call | tf_op jit(solution)/shard_map/pair_last/pallas_call | solution.py:489
Async XLA Ops:
  24.8 1.7 %collective-permute-start = (bf16[8,2,16,512]{3,2,1,0:T(8,128)(2,1)S(1)}, bf16[8,2,16,512]{3,2,1,0:T(8,128)(2,1)S(1)}, u32[]{:S(2)}, u32[]{:S(2)}) collective-permute-start(bf16[8,2,16,512]{3,2,1,0:T(8,128)(2,1)S(1)} %get-tuple-element.10.src_ref), channel_id=1, source_target_pairs={{0,2},{2,0},{4,6},{6,4},{8,10},{10,8},{12,14},{14,12},{16,18},{18,... | collective-permute-start | bytes 786440 | tf_op jit(solution)/shard_map/ppermute | solution.py:554

commit v4 on v3

--- a/solution.py
+++ b/solution.py
@@ -23,7 +23,7 @@
 HALF = LO // 128
 PAIRS = PH // 2
 EARLY = 8
-GROUPS = (8, 4)
+GROUPS = (8, 8)
 TABLE_ROWS = 2048
 
 NT = (((1,), (1,)), ((), ()))
@@ -398,10 +398,6 @@
         place = (1 - core) * share
     wide_ref[...] = src_ref[...].astype(F32)
 
-    def finished(first):
-        if last:
-            write(out_ref.at[pl.ds(first, group_size)], place + first, group_size)
-
     def cross(first, pair_ref):
         for p in range(PAIRS):
             for part in range(2):
@@ -453,6 +449,8 @@
                     im.append(c * v + d * u)
                 for n, value in enumerate(gather_lags(ends, re, im)):
                     out_ref[first + s, :, LO * n + lo : LO * n + lo + 128] = value
+            if last:
+                write(out_ref.at[pl.ds(first + s, 1)], place + first + s, 1)
 
     steps = share // group_size
     pairs, lagged = (pair_a, pair_b), (lag_a, lag_b)
@@ -463,9 +461,7 @@
             cross((i + 1) * group_size, pairs[(i + 1) % 2])
         if i:
             lags((i - 1) * group_size, lagged[(i - 1) % 2])
-            finished((i - 1) * group_size)
     lags((steps - 1) * group_size, lagged[(steps - 1) % 2])
-    finished((steps - 1) * group_size)
     for copy in copies:
         copy.wait()
 
@@ -484,7 +480,7 @@
     if last:
         scratch += [
             pltpu.VMEM((share, chans, SEG), F32),
-            pltpu.SemaphoreType.DMA((1 + share // group_size,)),
+            pltpu.SemaphoreType.DMA((1 + share,)),
         ]
     return pl.pallas_call(
         functools.partial(pair_kernel, last, group_size),

time: 28.9 us -> 28.8 us (level)
  no operation moved by 1% of the time
where the time goes in v4:
time: 28.8 us; the launch traced here: 28.5 us
  blocking collectives  19 us (66%)
  Pallas kernels  8.37 us (29%)
  between operations  0.68 us (2%)
  starting transfers between devices  0.45 us (2%)
    all_to_all x1, blocking collectives, local(): lax.all_to_all(packed, ('file', 'win'), split_axis=0, concat_axis=0, tile...  19 us
    pallas_call x2, Pallas kernels, pair_call(): pl.pallas_call(functools.partial(pair_kernel, last, group_size), in_specs...  3.24 us
    pallas_call x1, Pallas kernels, local(): pl.pallas_call(functools.partial(forward_kernel, files, wins, chans, scal...  2.71 us
    pallas_call x1, Pallas kernels, local(): pl.pallas_call(functools.partial(decimate_kernel, files, wins), out_shape...  2.42 us
  transfers between devices with their start and end apart: 1, of which 0 were waited for; matrix products, arithmetic and copies ran while one was open for 0% of the time, Pallas kernels for 4%

profile of v4, /device:TPU:0, one launch (start us, length us, event | category | flops | bytes accessed | tf_op | source)
XLA Modules:
  0.0 28.5 jit_solution(9570193558156130844)
XLA Ops:
  0.7 2.4 %decimate.1 = bf16[32,40,128]{2,1,0:T(8,128)(2,1)} custom-call(s32[1,1]{1,0:T(1,128)S(6)} %copy.6.offset_hbm, f32[1,64]{1,0:T(1,128)} %bitcast.4, s32[1,64]{1,0:T(1,128)} %bitcast.5, bf16[128,1280]{1,0:T(8,128)(2,1)} %bitcast.3), custom_call_target="tpu_custom_call" | custom-call | tf_op jit(solution)/shard_map/decimate/pallas_call | solution.py:513
  3.1 19.0 %all_to_all.5.data_ref = bf16[32,40,128]{2,1,0:T(8,128)(2,1)S(1)} all-to-all(bf16[32,40,128]{2,1,0:T(8,128)(2,1)} %decimate.1), channel_id=1, replica_groups=mesh['file'=16,'win'=2] {'file','win'}, dimensions={0} | all-to-all | bytes 655360 | tf_op jit(solution)/shard_map/all_to_all | solution.py:528
  22.1 2.7 %forward.1 = (f32[8,2,8,512]{3,2,1,0:T(8,128)S(1)}, bf16[8,2,16,512]{3,2,1,0:T(8,128)(2,1)S(1)}, bf16[1024,512]{1,0:T(8,128)(2,1)S(1)}, f32[2,8,8,256]{3,2,1,0:T(8,128)S(1)}) custom-call(bf16[32,40,128]{2,1,0:T(8,128)(2,1)S(1)} %all_to_all.5.data_ref, bf16[2048,512]{1,0:T(8,128)(2,1)} %constant.2.clone.table_hbm), custom_call_target="tpu_custom_call" | custom-call | tf_op jit(solution)/shard_map/forward/pallas_call | solution.py:529
  24.8 0.5 %collective-permute-start = (bf16[8,2,16,512]{3,2,1,0:T(8,128)(2,1)S(1)}, bf16[8,2,16,512]{3,2,1,0:T(8,128)(2,1)S(1)}, u32[]{:S(2)}, u32[]{:S(2)}) collective-permute-start(bf16[8,2,16,512]{3,2,1,0:T(8,128)(2,1)S(1)} %get-tuple-element.10.src_ref), channel_id=1, source_target_pairs={{0,2},{2,0},{4,6},{6,4},{8,10},{10,8},{12,14},{14,12},{16,18},{18,... | collective-permute-start | bytes 786440 | tf_op jit(solution)/shard_map/ppermute | solution.py:550
  25.3 1.2 %pair_first.1.refs_0_ = f32[16,8,2048]{2,1,0:T(8,128)S(1)} custom-call(f32[8,2,8,512]{3,2,1,0:T(8,128)S(1)} %get-tuple-element.9.own_ref, bf16[8,2,16,512]{3,2,1,0:T(8,128)(2,1)S(1)} %get-tuple-element.10.src_ref, bf16[1024,512]{1,0:T(8,128)(2,1)S(1)} %get-tuple-element.11.table_ref, f32[2,8,8,256]{3,2,1,0:T(8,128)S(1)} %get-tuple-element.12.turn_ref), custom_call_target="tpu_custom_call" | custom-call | tf_op jit(solution)/shard_map/pair_first/pallas_call | solution.py:485
  26.5 0.0 collective-permute-done.src_ref
  26.5 2.0 %pair_last.1 = f32[32,8,2048]{2,1,0:T(8,128)} custom-call(f32[8,2,8,512]{3,2,1,0:T(8,128)S(1)} %get-tuple-element.9.own_ref, bf16[8,2,16,512]{3,2,1,0:T(8,128)(2,1)S(1)} %collective-permute-done.src_ref, bf16[1024,512]{1,0:T(8,128)(2,1)S(1)} %get-tuple-element.11.table_ref, f32[2,8,8,256]{3,2,1,0:T(8,128)S(1)} %get-tuple-element.12.turn_ref, ...), custom_call_target="tpu_custom_call" | custom-call | tf_op jit(solution)/shard_map/pair_last/pallas_call | solution.py:485
Async XLA Ops:
  24.8 1.7 %collective-permute-start = (bf16[8,2,16,512]{3,2,1,0:T(8,128)(2,1)S(1)}, bf16[8,2,16,512]{3,2,1,0:T(8,128)(2,1)S(1)}, u32[]{:S(2)}, u32[]{:S(2)}) collective-permute-start(bf16[8,2,16,512]{3,2,1,0:T(8,128)(2,1)S(1)} %get-tuple-element.10.src_ref), channel_id=1, source_target_pairs={{0,2},{2,0},{4,6},{6,4},{8,10},{10,8},{12,14},{14,12},{16,18},{18,... | collective-permute-start | bytes 786440 | tf_op jit(solution)/shard_map/ppermute | solution.py:550

commit v5 on v4

--- a/solution.py
+++ b/solution.py
@@ -23,7 +23,7 @@
 HALF = LO // 128
 PAIRS = PH // 2
 EARLY = 8
-GROUPS = (8, 8)
+GROUPS = (16, 8)
 TABLE_ROWS = 2048
 
 NT = (((1,), (1,)), ((), ()))

time: 28.8 us -> 28.7 us (level)
  transfers between devices with their start and end apart: 1 -> 1, of which waited for: 0 -> 1; matrix products, arithmetic and copies ran while one was open for 0% -> 0% of each run, Pallas kernels for 4% -> 4%
where the time goes in v5:
time: 28.7 us; the launch traced here: 28.5 us
  blocking collectives  19 us (66%)
  Pallas kernels  8.24 us (29%)
  between operations  0.68 us (2%)
  starting transfers between devices  0.45 us (2%)
    all_to_all x1, blocking collectives, local(): lax.all_to_all(packed, ('file', 'win'), split_axis=0, concat_axis=0, tile...  19 us
    pallas_call x2, Pallas kernels, pair_call(): pl.pallas_call(functools.partial(pair_kernel, last, group_size), in_specs...  3.11 us
    pallas_call x1, Pallas kernels, local(): pl.pallas_call(functools.partial(forward_kernel, files, wins, chans, scal...  2.71 us
    pallas_call x1, Pallas kernels, local(): pl.pallas_call(functools.partial(decimate_kernel, files, wins), out_shape...  2.42 us
  transfers between devices with their start and end apart: 1, of which 1 were waited for; matrix products, arithmetic and copies ran while one was open for 0% of the time, Pallas kernels for 4%

profile of v5, /device:TPU:0, one launch (start us, length us, event | category | flops | bytes accessed | tf_op | source)
XLA Modules:
  0.0 28.5 jit_solution(14241926590193404355)
XLA Ops:
  0.7 2.4 %decimate.1 = bf16[32,40,128]{2,1,0:T(8,128)(2,1)} custom-call(s32[1,1]{1,0:T(1,128)S(6)} %copy.6.offset_hbm, f32[1,64]{1,0:T(1,128)} %bitcast.4, s32[1,64]{1,0:T(1,128)} %bitcast.5, bf16[128,1280]{1,0:T(8,128)(2,1)} %bitcast.3), custom_call_target="tpu_custom_call" | custom-call | tf_op jit(solution)/shard_map/decimate/pallas_call | solution.py:513
  3.1 19.0 %all_to_all.5.data_ref = bf16[32,40,128]{2,1,0:T(8,128)(2,1)S(1)} all-to-all(bf16[32,40,128]{2,1,0:T(8,128)(2,1)} %decimate.1), channel_id=1, replica_groups=mesh['file'=16,'win'=2] {'file','win'}, dimensions={0} | all-to-all | bytes 655360 | tf_op jit(solution)/shard_map/all_to_all | solution.py:528
  22.1 2.7 %forward.1 = (f32[8,2,8,512]{3,2,1,0:T(8,128)S(1)}, bf16[8,2,16,512]{3,2,1,0:T(8,128)(2,1)S(1)}, bf16[1024,512]{1,0:T(8,128)(2,1)S(1)}, f32[2,8,8,256]{3,2,1,0:T(8,128)S(1)}) custom-call(bf16[32,40,128]{2,1,0:T(8,128)(2,1)S(1)} %all_to_all.5.data_ref, bf16[2048,512]{1,0:T(8,128)(2,1)} %constant.2.clone.table_hbm), custom_call_target="tpu_custom_call" | custom-call | tf_op jit(solution)/shard_map/forward/pallas_call | solution.py:529
  24.8 0.5 %collective-permute-start = (bf16[8,2,16,512]{3,2,1,0:T(8,128)(2,1)S(1)}, bf16[8,2,16,512]{3,2,1,0:T(8,128)(2,1)S(1)}, u32[]{:S(2)}, u32[]{:S(2)}) collective-permute-start(bf16[8,2,16,512]{3,2,1,0:T(8,128)(2,1)S(1)} %get-tuple-element.10.src_ref), channel_id=1, source_target_pairs={{0,2},{2,0},{4,6},{6,4},{8,10},{10,8},{12,14},{14,12},{16,18},{18,... | collective-permute-start | bytes 786440 | tf_op jit(solution)/shard_map/ppermute | solution.py:550
  25.3 1.1 %pair_first.1.refs_0_ = f32[16,8,2048]{2,1,0:T(8,128)S(1)} custom-call(f32[8,2,8,512]{3,2,1,0:T(8,128)S(1)} %get-tuple-element.9.own_ref, bf16[8,2,16,512]{3,2,1,0:T(8,128)(2,1)S(1)} %get-tuple-element.10.src_ref, bf16[1024,512]{1,0:T(8,128)(2,1)S(1)} %get-tuple-element.11.table_ref, f32[2,8,8,256]{3,2,1,0:T(8,128)S(1)} %get-tuple-element.12.turn_ref), custom_call_target="tpu_custom_call" | custom-call | tf_op jit(solution)/shard_map/pair_first/pallas_call | solution.py:485
  26.4 0.1 collective-permute-done.src_ref
  26.4 2.0 %pair_last.1 = f32[32,8,2048]{2,1,0:T(8,128)} custom-call(f32[8,2,8,512]{3,2,1,0:T(8,128)S(1)} %get-tuple-element.9.own_ref, bf16[8,2,16,512]{3,2,1,0:T(8,128)(2,1)S(1)} %collective-permute-done.src_ref, bf16[1024,512]{1,0:T(8,128)(2,1)S(1)} %get-tuple-element.11.table_ref, f32[2,8,8,256]{3,2,1,0:T(8,128)S(1)} %get-tuple-element.12.turn_ref, ...), custom_call_target="tpu_custom_call" | custom-call | tf_op jit(solution)/shard_map/pair_last/pallas_call | solution.py:485
Async XLA Ops:
  24.8 1.6 %collective-permute-start = (bf16[8,2,16,512]{3,2,1,0:T(8,128)(2,1)S(1)}, bf16[8,2,16,512]{3,2,1,0:T(8,128)(2,1)S(1)}, u32[]{:S(2)}, u32[]{:S(2)}) collective-permute-start(bf16[8,2,16,512]{3,2,1,0:T(8,128)(2,1)S(1)} %get-tuple-element.10.src_ref), channel_id=1, source_target_pairs={{0,2},{2,0},{4,6},{6,4},{8,10},{10,8},{12,14},{14,12},{16,18},{18,... | collective-permute-start | bytes 786440 | tf_op jit(solution)/shard_map/ppermute | solution.py:550

commit v6 on v4

--- a/solution.py
+++ b/solution.py
@@ -183,7 +183,7 @@
 def forward_kernel(
     files, wins, chans, scale,
     data_ref, table_hbm, own_ref, src_ref, table_ref, turn_ref,
-    waves_ref, fixed_ref, high_ref, low_ref, spec_ref, sems,
+    waves_ref, fixed_ref, split_ref, spec_ref, sems,
 ):
     copies = [
         pltpu.make_async_copy(source, target, sems.at[i])
@@ -275,8 +275,8 @@
                     for part, value in enumerate((re, im)):
                         at = slice(128 * h, 128 * h + 128)
                         high, low = split(value)
-                        high_ref[part, p, base : base + rows, at] = high
-                        low_ref[part, p, base : base + rows, at] = low
+                        split_ref[0, part, p, base : base + rows, at] = high
+                        split_ref[1, part, p, base : base + rows, at] = low
     groups = wins * segs
     count = groups * rows
     copies[0].wait()
@@ -285,8 +285,8 @@
     def product(part, first, last, begin, end):
         lines = (last - first) * count
         return three_pass(
-            high_ref[part, first:last].reshape(lines, LO),
-            low_ref[part, first:last].reshape(lines, LO),
+            split_ref[0, part, first:last].reshape(lines, LO),
+            split_ref[1, part, first:last].reshape(lines, LO),
             waves_ref[begin * NA : end * NA, :LO],
             waves_ref[begin * NA : end * NA, LO:],
             NT,
@@ -296,8 +296,13 @@
         value = product(part, 0, 1, begin, begin + 2)[0]
         spec_ref[0, :, 2 * NA * part : 2 * NA * part + NA] = value[:, :NA]
         spec_ref[0, :, 2 * NA * part + NA : 2 * NA * (part + 1)] = -value[:, NA:]
-    of_re = product(0, 1, PAIRS, 0, 4)
-    of_im = product(1, 1, PAIRS, 0, 4)
+    dot = functools.partial(lax.dot_general, dimension_numbers=NT, preferred_element_type=F32)
+    lines = 2 * (PAIRS - 1) * count
+    table = waves_ref[: 4 * NA, :LO]
+    both = dot(split_ref[:, :, 1:].reshape(2 * lines, LO), table)
+    rest = dot(split_ref[0, :, 1:].reshape(lines, LO), waves_ref[: 4 * NA, LO:])
+    of_both = (both[:lines] + (both[lines:] + rest)).reshape(2, PAIRS - 1, count, 4 * NA)
+    of_re, of_im = of_both[0], of_both[1]
     c, s, cc, ss = (slice(NA * i, NA * (i + 1)) for i in range(4))
     spec_ref[1:, :, c] = of_re[..., c] + of_im[..., s]
     spec_ref[1:, :, s] = of_im[..., c] - of_re[..., s]
@@ -539,8 +544,7 @@
         scratch_shapes=[
             pltpu.VMEM((6 * NA, 2 * LO), BF16),
             pltpu.VMEM((files * wins, rows, TD), F32),
-            pltpu.VMEM((2, PAIRS, groups * rows, LO), BF16),
-            pltpu.VMEM((2, PAIRS, groups * rows, LO), BF16),
+            pltpu.VMEM((2, 2, PAIRS, groups * rows, LO), BF16),
             pltpu.VMEM((PAIRS, groups * rows, 4 * NA), F32),
             pltpu.SemaphoreType.DMA((2,)),
         ],

time: 28.8 us -> 28.8 us (level)
  no operation moved by 1% of the time
where the time goes in v6:
time: 28.8 us; the launch traced here: 28.6 us
  blocking collectives  19 us (66%)
  Pallas kernels  8.4 us (29%)
  between operations  0.68 us (2%)
  starting transfers between devices  0.44 us (2%)
    all_to_all x1, blocking collectives, local(): lax.all_to_all(packed, ('file', 'win'), split_axis=0, concat_axis=0, tile...  19 us
    pallas_call x2, Pallas kernels, pair_call(): pl.pallas_call(functools.partial(pair_kernel, last, group_size), in_specs...  3.24 us
    pallas_call x1, Pallas kernels, local(): pl.pallas_call(functools.partial(forward_kernel, files, wins, chans, scal...  2.73 us
    pallas_call x1, Pallas kernels, local(): pl.pallas_call(functools.partial(decimate_kernel, files, wins), out_shape...  2.42 us
  transfers between devices with their start and end apart: 1, of which 0 were waited for; matrix products, arithmetic and copies ran while one was open for 0% of the time, Pallas kernels for 4%

profile of v6, /device:TPU:0, one launch (start us, length us, event | category | flops | bytes accessed | tf_op | source)
XLA Modules:
  0.0 28.6 jit_solution(4804482269123313661)
XLA Ops:
  0.7 2.4 %decimate.1 = bf16[32,40,128]{2,1,0:T(8,128)(2,1)} custom-call(s32[1,1]{1,0:T(1,128)S(6)} %copy.6.offset_hbm, f32[1,64]{1,0:T(1,128)} %bitcast.4, s32[1,64]{1,0:T(1,128)} %bitcast.5, bf16[128,1280]{1,0:T(8,128)(2,1)} %bitcast.3), custom_call_target="tpu_custom_call" | custom-call | tf_op jit(solution)/shard_map/decimate/pallas_call | solution.py:518
  3.1 19.0 %all_to_all.5.data_ref = bf16[32,40,128]{2,1,0:T(8,128)(2,1)S(1)} all-to-all(bf16[32,40,128]{2,1,0:T(8,128)(2,1)} %decimate.1), channel_id=1, replica_groups=mesh['file'=16,'win'=2] {'file','win'}, dimensions={0} | all-to-all | bytes 655360 | tf_op jit(solution)/shard_map/all_to_all | solution.py:533
  22.1 2.7 %forward.1 = (f32[8,2,8,512]{3,2,1,0:T(8,128)S(1)}, bf16[8,2,16,512]{3,2,1,0:T(8,128)(2,1)S(1)}, bf16[1024,512]{1,0:T(8,128)(2,1)S(1)}, f32[2,8,8,256]{3,2,1,0:T(8,128)S(1)}) custom-call(bf16[32,40,128]{2,1,0:T(8,128)(2,1)S(1)} %all_to_all.5.data_ref, bf16[2048,512]{1,0:T(8,128)(2,1)} %constant.2.clone.table_hbm), custom_call_target="tpu_custom_call" | custom-call | tf_op jit(solution)/shard_map/forward/pallas_call | solution.py:534
  24.9 0.4 %collective-permute-start = (bf16[8,2,16,512]{3,2,1,0:T(8,128)(2,1)S(1)}, bf16[8,2,16,512]{3,2,1,0:T(8,128)(2,1)S(1)}, u32[]{:S(2)}, u32[]{:S(2)}) collective-permute-start(bf16[8,2,16,512]{3,2,1,0:T(8,128)(2,1)S(1)} %get-tuple-element.10.src_ref), channel_id=1, source_target_pairs={{0,2},{2,0},{4,6},{6,4},{8,10},{10,8},{12,14},{14,12},{16,18},{18,... | collective-permute-start | bytes 786440 | tf_op jit(solution)/shard_map/ppermute | solution.py:554
  25.3 1.2 %pair_first.1.refs_0_ = f32[16,8,2048]{2,1,0:T(8,128)S(1)} custom-call(f32[8,2,8,512]{3,2,1,0:T(8,128)S(1)} %get-tuple-element.9.own_ref, bf16[8,2,16,512]{3,2,1,0:T(8,128)(2,1)S(1)} %get-tuple-element.10.src_ref, bf16[1024,512]{1,0:T(8,128)(2,1)S(1)} %get-tuple-element.11.table_ref, f32[2,8,8,256]{3,2,1,0:T(8,128)S(1)} %get-tuple-element.12.turn_ref), custom_call_target="tpu_custom_call" | custom-call | tf_op jit(solution)/shard_map/pair_first/pallas_call | solution.py:490
  26.5 0.0 collective-permute-done.src_ref
  26.5 2.0 %pair_last.1 = f32[32,8,2048]{2,1,0:T(8,128)} custom-call(f32[8,2,8,512]{3,2,1,0:T(8,128)S(1)} %get-tuple-element.9.own_ref, bf16[8,2,16,512]{3,2,1,0:T(8,128)(2,1)S(1)} %collective-permute-done.src_ref, bf16[1024,512]{1,0:T(8,128)(2,1)S(1)} %get-tuple-element.11.table_ref, f32[2,8,8,256]{3,2,1,0:T(8,128)S(1)} %get-tuple-element.12.turn_ref, ...), custom_call_target="tpu_custom_call" | custom-call | tf_op jit(solution)/shard_map/pair_last/pallas_call | solution.py:490
Async XLA Ops:
  24.9 1.7 %collective-permute-start = (bf16[8,2,16,512]{3,2,1,0:T(8,128)(2,1)S(1)}, bf16[8,2,16,512]{3,2,1,0:T(8,128)(2,1)S(1)}, u32[]{:S(2)}, u32[]{:S(2)}) collective-permute-start(bf16[8,2,16,512]{3,2,1,0:T(8,128)(2,1)S(1)} %get-tuple-element.10.src_ref), channel_id=1, source_target_pairs={{0,2},{2,0},{4,6},{6,4},{8,10},{10,8},{12,14},{14,12},{16,18},{18,... | collective-permute-start | bytes 786440 | tf_op jit(solution)/shard_map/ppermute | solution.py:554
